TPU v7x, 128 devices: a whole 4x4x4 slice. The times are simulated.
128 devices in a mesh: head: 8 (over y_hi, z), inner: 4 (over y_lo, core), outer: 4 (over x).
Axes of the slice: x: 4, y: 4 (y_hi: 2, y_lo: 2; y = y_hi * 2 + y_lo), z: 4, core: 2. Of those that a mesh axis runs over, the one named last changes fastest.
Arguments:
- queries: bfloat16 [16384, 2048], P(('head', 'inner', 'outer')), may hold values from -18 to 18
- keys: bfloat16 [16384, 1024], P(('head', 'inner', 'outer')), may hold values from -6 to 6
- values: bfloat16 [16384, 1024], P(('head', 'inner', 'outer')), may hold values from -6 to 6
- output: bfloat16 [16384, 2048], P(('head', 'inner', 'outer')), may hold values from -6 to 6
- grad_output: bfloat16 [16384, 2048], P(('head', 'inner', 'outer')), may hold values from -6 to 6
- positions: int32 [16384], P(('head', 'inner', 'outer')), may hold values from 0 to 16383, as said below
Outputs:
- grad_queries: bfloat16 [16384, 2048], P(('head', 'inner', 'outer'))
- grad_keys: bfloat16 [16384, 1024], P(('head', 'inner', 'outer'))
- grad_values: bfloat16 [16384, 1024], P(('head', 'inner', 'outer'))
Inputs may be any that keep to these rules, and one draw needn't show every extreme that they name: positions form a permutation of 0 to 16383.
All inputs are finite; a program needn't handle non-finite values.
Results may differ from a plain program's by a relative error of at most 0.0049.
Values may be sent and summed in bfloat16 or wider, within the bound.
A program may use at most 64 MiB of HBM per device.

v0:
```python
import jax
import jax.numpy as jnp
from jax import lax
from jax.sharding import PartitionSpec as P

HD = 128
QH_DEV = 2


soft_cap = 50.0
query_scale = 1.0 / 12.0


def shifted(value, axis, steps):
    count = lax.axis_size(axis)
    pairs = [(source, (source + steps) % count) for source in range(count)]
    return lax.ppermute(value, axis, pairs)


def capped(query_tile, key_tile):
    raw_scores = jnp.einsum("qed,kd->eqk", query_tile, key_tile, preferred_element_type=jnp.float32)
    tanh_part = jnp.tanh(raw_scores * (query_scale / soft_cap))
    return (soft_cap * tanh_part, tanh_part)


def tile_sums(query_tile, query_pos, key_tile, key_pos):

    def active_tile(unused):
        scores, tanh_part = capped(query_tile, key_tile)
        causal = (key_pos[None, :] <= query_pos[:, None])[None]
        return jnp.sum(jnp.where(causal, jnp.exp(scores), 0.0), axis=2)

    def skipped(unused):
        return jnp.zeros((query_tile.shape[1], query_tile.shape[0]), jnp.float32)

    return lax.cond(jnp.min(key_pos) <= jnp.max(query_pos), active_tile, skipped, 0)


def tile_grads(
    query_tile, dout_tile, query_pos, log_tile, delta_tile, key_tile, value_tile, key_pos
):

    def active_tile(unused):
        scores, tanh_part = capped(query_tile, key_tile)
        causal = (key_pos[None, :] <= query_pos[:, None])[None]
        weights = jnp.where(causal, jnp.exp(scores - log_tile[:, :, None]), 0.0)
        weights_low = weights.astype(jnp.bfloat16)
        value_part = jnp.einsum(
            "eqk,qed->kd", weights_low, dout_tile, preferred_element_type=jnp.float32
        )
        grad_weights = jnp.einsum(
            "qed,kd->eqk", dout_tile, value_tile, preferred_element_type=jnp.float32
        )
        grad_scores = (
            weights
            * (grad_weights - delta_tile.T[:, :, None])
            * (1.0 - tanh_part * tanh_part)
            * query_scale
        ).astype(jnp.bfloat16)
        query_part = jnp.einsum(
            "eqk,kd->qed", grad_scores, key_tile, preferred_element_type=jnp.float32
        )
        key_part = jnp.einsum(
            "eqk,qed->kd", grad_scores, query_tile, preferred_element_type=jnp.float32
        )
        return (query_part, key_part, value_part)

    def skipped(unused):
        query_part = jnp.zeros(query_tile.shape, jnp.float32)
        key_part = jnp.zeros(key_tile.shape, jnp.float32)
        return (query_part, key_part, key_part)

    return lax.cond(jnp.min(key_pos) <= jnp.max(query_pos), active_tile, skipped, 0)


def local(queries, keys, values, output, grad_output, positions):
    row_count = queries.shape[0]
    feature_cols = grad_output.shape[1]
    delta_rows = jnp.sum(
        (grad_output.astype(jnp.float32) * output.astype(jnp.float32)).reshape(
            row_count, feature_cols // HD, HD
        ),
        axis=2,
    )
    query_local, key_local, value_local, dout_local = (
        lax.all_to_all(queries, "head", split_axis=1, concat_axis=0, tiled=True),
        lax.all_to_all(keys, "head", split_axis=1, concat_axis=0, tiled=True),
        lax.all_to_all(values, "head", split_axis=1, concat_axis=0, tiled=True),
        lax.all_to_all(grad_output, "head", split_axis=1, concat_axis=0, tiled=True),
    )
    delta_local = lax.all_to_all(delta_rows, "head", split_axis=1, concat_axis=0, tiled=True)
    every_pos = lax.all_gather(positions, ("head", "inner", "outer"), axis=0, tiled=True)
    head_count = lax.axis_size("head")
    cycle_count = lax.axis_size(("inner", "outer"))
    ctx_rows = query_local.shape[0]
    ctx_pos = (
        every_pos.reshape(head_count, cycle_count, row_count)
        .transpose(1, 0, 2)
        .reshape(cycle_count * ctx_rows)
    )
    my_place = lax.axis_index(("inner", "outer"))
    my_pos = lax.dynamic_slice_in_dim(ctx_pos, my_place * ctx_rows, ctx_rows, 0)
    query_heads = query_local.reshape(ctx_rows, QH_DEV, HD)
    dout_heads = dout_local.reshape(ctx_rows, QH_DEV, HD)
    tile_rows = min(512, ctx_rows // 2)
    tile_count = ctx_rows // tile_rows
    key_rows = lax.all_gather(key_local, ("inner", "outer"), axis=0, tiled=True)
    piece_rows = key_rows.shape[0]
    key_span = 512

    def one_tile(tile_idx, acc):
        key_tile = lax.dynamic_slice_in_dim(key_rows, tile_idx * key_span, key_span, 0)
        key_pos = lax.dynamic_slice_in_dim(ctx_pos, tile_idx * key_span, key_span, 0)
        partial_value = []
        for query_idx in range(tile_count):
            rows_here = slice(query_idx * tile_rows, (query_idx + 1) * tile_rows)
            partial_value.append(
                tile_sums(query_heads[rows_here], my_pos[rows_here], key_tile, key_pos)
            )
        return acc + jnp.concatenate(partial_value, axis=1)

    exp_sums = lax.fori_loop(
        0, piece_rows // key_span, one_tile, jnp.zeros((QH_DEV, ctx_rows), jnp.float32)
    )
    log_sums = jnp.log(exp_sums)

    def visit_block(kv_pair, key_pos, kv_grads, query_grad):
        query_parts = [
            query_grad[query_idx * tile_rows : (query_idx + 1) * tile_rows]
            for query_idx in range(tile_count)
        ]
        key_parts = []
        value_parts = []
        for key_idx in range(tile_count):
            key_here = slice(key_idx * tile_rows, (key_idx + 1) * tile_rows)
            key_sum = jnp.zeros((tile_rows, HD), jnp.float32)
            value_sum = jnp.zeros((tile_rows, HD), jnp.float32)
            for query_idx in range(tile_count):
                rows_here = slice(query_idx * tile_rows, (query_idx + 1) * tile_rows)
                query_part, key_part, value_part = tile_grads(
                    query_heads[rows_here],
                    dout_heads[rows_here],
                    my_pos[rows_here],
                    log_sums[:, rows_here],
                    delta_local[rows_here],
                    kv_pair[0, key_here],
                    kv_pair[1, key_here],
                    key_pos[key_here],
                )
                query_parts[query_idx] = query_parts[query_idx] + query_part
                key_sum = key_sum + key_part
                value_sum = value_sum + value_part
            key_parts.append(key_sum)
            value_parts.append(value_sum)
        kv_grads = kv_grads + jnp.stack(
            [jnp.concatenate(key_parts, axis=0), jnp.concatenate(value_parts, axis=0)]
        )
        return (kv_grads, jnp.concatenate(query_parts, axis=0))

    start_grads = jnp.zeros((2, ctx_rows, HD), jnp.float32)
    start_query = jnp.zeros((ctx_rows, QH_DEV, HD), jnp.float32)
    kv_start = jnp.stack([key_local, value_local])

    def cycle_step(step_idx, state):
        kv_pair, kv_grads, query_grad = state
        block_id = (my_place - step_idx) % cycle_count
        key_pos = lax.dynamic_slice_in_dim(ctx_pos, block_id * ctx_rows, ctx_rows, 0)
        kv_grads, query_grad = visit_block(kv_pair, key_pos, kv_grads, query_grad)
        kv_pair = shifted(kv_pair, ("inner", "outer"), 1)
        kv_grads = shifted(kv_grads, ("inner", "outer"), 1)
        return (kv_pair, kv_grads, query_grad)

    finished = lax.fori_loop(0, cycle_count, cycle_step, (kv_start, start_grads, start_query))
    kv_home, kv_grads, query_grad = finished
    query_low = query_grad.reshape(ctx_rows, QH_DEV * HD).astype(jnp.bfloat16)
    key_low = kv_grads[0].astype(jnp.bfloat16)
    value_low = kv_grads[1].astype(jnp.bfloat16)
    grad_queries, grad_keys, grad_values = (
        lax.all_to_all(query_low, "head", split_axis=0, concat_axis=1, tiled=True),
        lax.all_to_all(key_low, "head", split_axis=0, concat_axis=1, tiled=True),
        lax.all_to_all(value_low, "head", split_axis=0, concat_axis=1, tiled=True),
    )
    return (grad_queries, grad_keys, grad_values)


def solution(mesh):
    return jax.shard_map(
        local,
        mesh=mesh,
        in_specs=(
            P(("head", "inner", "outer"), None),
            P(("head", "inner", "outer"), None),
            P(("head", "inner", "outer"), None),
            P(("head", "inner", "outer"), None),
            P(("head", "inner", "outer"), None),
            P(("head", "inner", "outer")),
        ),
        out_specs=(
            P(("head", "inner", "outer"), None),
            P(("head", "inner", "outer"), None),
            P(("head", "inner", "outer"), None),
        ),
        check_vma=False,
    )
```

profile of v0, /device:TPU:64, one launch (start us, length us, event | category | flops | bytes accessed | tf_op | source)
XLA Modules:
  0.0 1628.5 jit_solution(544799269484227100)
XLA Ops:
  8.2 13.7 all_to_all.134
  30.6 6.3 all-to-all-done.1
  42.2 231.9 %all-gather = s32[128,1,128]{2,1,0:T(1,128)S(1)} all-gather(s32[1,1,128]{2,1,0:T(1,128)S(1)} %bitcast.284), channel_id=1, replica_groups=mesh['head'=8,'inner'=4,'outer'=4] {'head','inner','outer'}, dimensions={0}, use_global_device_ids=true | all-gather | bytes 66048 | tf_op jit(solution)/shard_map/all_gather | solution.py:92
  275.2 84.0 %all-to-all-start.3 = ((bf16[128,8,256]{0,2,1:T(8,128)(2,1)}), bf16[128,8,256]{0,2,1:T(8,128)(2,1)S(1)}, u32[]{:S(2)}, u32[]{:S(2)}) async-start(bf16[128,8,256]{0,2,1:T(8,128)(2,1)} %bitcast.57), calls=%async_computation.3 | async-start | bytes 1048576 | tf_op jit(solution)/shard_map/all_to_all | solution.py:89
  373.1 196.3 %while.35 = (s32[]{:T(128)}, f32[2,1024]{1,0:T(2,128)S(1)}, s32[16384]{0:T(1024)}, s32[]{:T(128)}, bf16[16384,128]{1,0:T(8,128)(2,1)}, /*index=5*/s32[1024]{0:T(...) while((s32[]{:T(128)}, f32[2,1024]{1,0:T(2,128)S(1)}, ...), condition=%wide.region_10.11_spmd.clone, body=%wide.region_2.10_spmd.clone.sunk | while | flops 273158656 | bytes 2150669 | solution.py:122
  571.6 1006.1 %while.34 = (s32[]{:T(128)}, bf16[2,1024,128]{2,1,0:T(8,128)(2,1)}, f32[2,1024,128]{2,1,0:T(8,128)}, f32[1024,2,128]{2,0,1:T(8,128)}, s32[]{:T(128)}, /*index=5*...) while((s32[]{:T(128)}, bf16[2,1024,128]{2,1,0:T(8,128)(2,1)}, ...), condition=%wide.region_23.24_spmd, body=%wide.region_12.23_spmd.sunk | while | flops 2720793600 | bytes 91088360 | solution.py:173
  606.3 21.7 %collective-permute-done = bf16[2,1024,128]{2,1,0:T(8,128)(2,1)} collective-permute-done((bf16[2,1024,128]{2,1,0:T(8,128)(2,1)S(1)}, bf16[2,1024,128]{2,1,0:T(8,128)(2,1)}, u32[]{:S(2)}, u32[]{:S(2)}) %collective-permute-start) | collective-permute-done | bytes 524320 | tf_op jit(solution)/shard_map/while/body/eval_jaxpr/ppermute | solution.py:17
  660.2 28.1 %collective-permute-done = bf16[2,1024,128]{2,1,0:T(8,128)(2,1)} collective-permute-done((bf16[2,1024,128]{2,1,0:T(8,128)(2,1)S(1)}, bf16[2,1024,128]{2,1,0:T(8,128)(2,1)}, u32[]{:S(2)}, u32[]{:S(2)}) %collective-permute-start) | collective-permute-done | bytes 524320 | tf_op jit(solution)/shard_map/while/body/eval_jaxpr/ppermute | solution.py:17
  719.4 28.1 %collective-permute-done = bf16[2,1024,128]{2,1,0:T(8,128)(2,1)} collective-permute-done((bf16[2,1024,128]{2,1,0:T(8,128)(2,1)S(1)}, bf16[2,1024,128]{2,1,0:T(8,128)(2,1)}, u32[]{:S(2)}, u32[]{:S(2)}) %collective-permute-start) | collective-permute-done | bytes 524320 | tf_op jit(solution)/shard_map/while/body/eval_jaxpr/ppermute | solution.py:17
  777.1 30.3 %collective-permute-done = bf16[2,1024,128]{2,1,0:T(8,128)(2,1)} collective-permute-done((bf16[2,1024,128]{2,1,0:T(8,128)(2,1)S(1)}, bf16[2,1024,128]{2,1,0:T(8,128)(2,1)}, u32[]{:S(2)}, u32[]{:S(2)}) %collective-permute-start) | collective-permute-done | bytes 524320 | tf_op jit(solution)/shard_map/while/body/eval_jaxpr/ppermute | solution.py:17
  836.9 31.6 %collective-permute-done = bf16[2,1024,128]{2,1,0:T(8,128)(2,1)} collective-permute-done((bf16[2,1024,128]{2,1,0:T(8,128)(2,1)S(1)}, bf16[2,1024,128]{2,1,0:T(8,128)(2,1)}, u32[]{:S(2)}, u32[]{:S(2)}) %collective-permute-start) | collective-permute-done | bytes 524320 | tf_op jit(solution)/shard_map/while/body/eval_jaxpr/ppermute | solution.py:17
  899.7 32.7 %collective-permute-done = bf16[2,1024,128]{2,1,0:T(8,128)(2,1)} collective-permute-done((bf16[2,1024,128]{2,1,0:T(8,128)(2,1)S(1)}, bf16[2,1024,128]{2,1,0:T(8,128)(2,1)}, u32[]{:S(2)}, u32[]{:S(2)}) %collective-permute-start) | collective-permute-done | bytes 524320 | tf_op jit(solution)/shard_map/while/body/eval_jaxpr/ppermute | solution.py:17
  963.5 34.8 %collective-permute-done = bf16[2,1024,128]{2,1,0:T(8,128)(2,1)} collective-permute-done((bf16[2,1024,128]{2,1,0:T(8,128)(2,1)S(1)}, bf16[2,1024,128]{2,1,0:T(8,128)(2,1)}, u32[]{:S(2)}, u32[]{:S(2)}) %collective-permute-start) | collective-permute-done | bytes 524320 | tf_op jit(solution)/shard_map/while/body/eval_jaxpr/ppermute | solution.py:17
  1029.5 35.1 %collective-permute-done = bf16[2,1024,128]{2,1,0:T(8,128)(2,1)} collective-permute-done((bf16[2,1024,128]{2,1,0:T(8,128)(2,1)S(1)}, bf16[2,1024,128]{2,1,0:T(8,128)(2,1)}, u32[]{:S(2)}, u32[]{:S(2)}) %collective-permute-start) | collective-permute-done | bytes 524320 | tf_op jit(solution)/shard_map/while/body/eval_jaxpr/ppermute | solution.py:17
  1095.7 34.2 %collective-permute-done = bf16[2,1024,128]{2,1,0:T(8,128)(2,1)} collective-permute-done((bf16[2,1024,128]{2,1,0:T(8,128)(2,1)S(1)}, bf16[2,1024,128]{2,1,0:T(8,128)(2,1)}, u32[]{:S(2)}, u32[]{:S(2)}) %collective-permute-start) | collective-permute-done | bytes 524320 | tf_op jit(solution)/shard_map/while/body/eval_jaxpr/ppermute | solution.py:17
  1161.0 31.6 %collective-permute-done = bf16[2,1024,128]{2,1,0:T(8,128)(2,1)} collective-permute-done((bf16[2,1024,128]{2,1,0:T(8,128)(2,1)S(1)}, bf16[2,1024,128]{2,1,0:T(8,128)(2,1)}, u32[]{:S(2)}, u32[]{:S(2)}) %collective-permute-start) | collective-permute-done | bytes 524320 | tf_op jit(solution)/shard_map/while/body/eval_jaxpr/ppermute | solution.py:17
  1223.7 32.7 %collective-permute-done = bf16[2,1024,128]{2,1,0:T(8,128)(2,1)} collective-permute-done((bf16[2,1024,128]{2,1,0:T(8,128)(2,1)S(1)}, bf16[2,1024,128]{2,1,0:T(8,128)(2,1)}, u32[]{:S(2)}, u32[]{:S(2)}) %collective-permute-start) | collective-permute-done | bytes 524320 | tf_op jit(solution)/shard_map/while/body/eval_jaxpr/ppermute | solution.py:17
  1287.5 33.2 %collective-permute-done = bf16[2,1024,128]{2,1,0:T(8,128)(2,1)} collective-permute-done((bf16[2,1024,128]{2,1,0:T(8,128)(2,1)S(1)}, bf16[2,1024,128]{2,1,0:T(8,128)(2,1)}, u32[]{:S(2)}, u32[]{:S(2)}) %collective-permute-start) | collective-permute-done | bytes 524320 | tf_op jit(solution)/shard_map/while/body/eval_jaxpr/ppermute | solution.py:17
  1351.9 32.8 %collective-permute-done = bf16[2,1024,128]{2,1,0:T(8,128)(2,1)} collective-permute-done((bf16[2,1024,128]{2,1,0:T(8,128)(2,1)S(1)}, bf16[2,1024,128]{2,1,0:T(8,128)(2,1)}, u32[]{:S(2)}, u32[]{:S(2)}) %collective-permute-start) | collective-permute-done | bytes 524320 | tf_op jit(solution)/shard_map/while/body/eval_jaxpr/ppermute | solution.py:17
  1414.3 35.2 %collective-permute-done = bf16[2,1024,128]{2,1,0:T(8,128)(2,1)} collective-permute-done((bf16[2,1024,128]{2,1,0:T(8,128)(2,1)S(1)}, bf16[2,1024,128]{2,1,0:T(8,128)(2,1)}, u32[]{:S(2)}, u32[]{:S(2)}) %collective-permute-start) | collective-permute-done | bytes 524320 | tf_op jit(solution)/shard_map/while/body/eval_jaxpr/ppermute | solution.py:17
  1480.6 34.3 %collective-permute-done = bf16[2,1024,128]{2,1,0:T(8,128)(2,1)} collective-permute-done((bf16[2,1024,128]{2,1,0:T(8,128)(2,1)S(1)}, bf16[2,1024,128]{2,1,0:T(8,128)(2,1)}, u32[]{:S(2)}, u32[]{:S(2)}) %collective-permute-start) | collective-permute-done | bytes 524320 | tf_op jit(solution)/shard_map/while/body/eval_jaxpr/ppermute | solution.py:17
  1546.0 31.7 %collective-permute-done = bf16[2,1024,128]{2,1,0:T(8,128)(2,1)} collective-permute-done((bf16[2,1024,128]{2,1,0:T(8,128)(2,1)S(1)}, bf16[2,1024,128]{2,1,0:T(8,128)(2,1)}, u32[]{:S(2)}, u32[]{:S(2)}) %collective-permute-start) | collective-permute-done | bytes 524320 | tf_op jit(solution)/shard_map/while/body/eval_jaxpr/ppermute | solution.py:17
  1579.8 14.5 all_to_all.135
  1594.3 6.7 all-to-all-start.7
  (1530 shorter events, 786.1 us)
Async XLA Ops:
  7.2 365.9 %all-gather.3.cloned.1.call-start = ((), (), s32[]{:S(2)}) async-start(), calls=%async_computation.8 | async-start | bytes 4456448 | tf_op jit(solution)/shard_map/all_gather | solution.py:107
  36.9 238.3 %all-to-all-start.2 = ((bf16[128,8,256]{0,2,1:T(8,128)(2,1)}), bf16[128,8,256]{0,2,1:T(8,128)(2,1)S(1)}, u32[]{:S(2)}, u32[]{:S(2)}) async-start(bf16[128,8,256]{0,2,1:T(8,128)(2,1)} %bitcast.54), calls=%async_computation.2 | async-start | bytes 1048576 | tf_op jit(solution)/shard_map/all_to_all | solution.py:86
  275.2 91.6 %all-to-all-start.3 = ((bf16[128,8,256]{0,2,1:T(8,128)(2,1)}), bf16[128,8,256]{0,2,1:T(8,128)(2,1)S(1)}, u32[]{:S(2)}, u32[]{:S(2)}) async-start(bf16[128,8,256]{0,2,1:T(8,128)(2,1)} %bitcast.57), calls=%async_computation.3 | async-start | bytes 1048576 | tf_op jit(solution)/shard_map/all_to_all | solution.py:89
  366.8 202.7 %all-to-all-start.4 = ((f32[128,8,2]{0,2,1:T(2,128)}), f32[128,8,2]{0,2,1:T(2,128)S(1)}, u32[]{:S(2)}, u32[]{:S(2)}) async-start(f32[128,8,2]{0,2,1:T(2,128)} %bitcast.59), calls=%async_computation.4 | async-start | bytes 16384 | tf_op jit(solution)/shard_map/all_to_all | solution.py:91
  897.2 35.1 %collective-permute-start.1 = (f32[2,1024,128]{2,1,0:T(8,128)}, f32[2,1024,128]{2,1,0:T(8,128)}, u32[]{:S(2)}, u32[]{:S(2)}) collective-permute-start(f32[2,1024,128]{2,1,0:T(8,128)} %maximum_add_fusion.4), channel_id=1, source_target_pairs={{0,1},{1,2},{2,3},{3,4},{4,5},{5,6},{6,7},{7,8},{8,9},{9,10},{10,1... | collective-permute-start | bytes 3145736 | tf_op jit(solution)/shard_map/while/body/eval_jaxpr/ppermute | solution.py:17
  897.2 35.1 %collective-permute-start = (bf16[2,1024,128]{2,1,0:T(8,128)(2,1)S(1)}, bf16[2,1024,128]{2,1,0:T(8,128)(2,1)}, u32[]{:S(2)}, u32[]{:S(2)}) collective-permute-start(bf16[2,1024,128]{2,1,0:T(8,128)(2,1)S(1)} %copy.139), channel_id=1, source_target_pairs={{0,1},{1,2},{2,3},{3,4},{4,5},{5,6},{6,7},{7,8},{8,9},{9,10},{10,1... | collective-permute-start | bytes 1572872 | tf_op jit(solution)/shard_map/while/body/eval_jaxpr/ppermute | solution.py:17
  961.1 37.3 %collective-permute-start.1 = (f32[2,1024,128]{2,1,0:T(8,128)}, f32[2,1024,128]{2,1,0:T(8,128)}, u32[]{:S(2)}, u32[]{:S(2)}) collective-permute-start(f32[2,1024,128]{2,1,0:T(8,128)} %maximum_add_fusion.4), channel_id=1, source_target_pairs={{0,1},{1,2},{2,3},{3,4},{4,5},{5,6},{6,7},{7,8},{8,9},{9,10},{10,1... | collective-permute-start | bytes 3145736 | tf_op jit(solution)/shard_map/while/body/eval_jaxpr/ppermute | solution.py:17
  961.1 37.3 %collective-permute-start = (bf16[2,1024,128]{2,1,0:T(8,128)(2,1)S(1)}, bf16[2,1024,128]{2,1,0:T(8,128)(2,1)}, u32[]{:S(2)}, u32[]{:S(2)}) collective-permute-start(bf16[2,1024,128]{2,1,0:T(8,128)(2,1)S(1)} %copy.139), channel_id=1, source_target_pairs={{0,1},{1,2},{2,3},{3,4},{4,5},{5,6},{6,7},{7,8},{8,9},{9,10},{10,1... | collective-permute-start | bytes 1572872 | tf_op jit(solution)/shard_map/while/body/eval_jaxpr/ppermute | solution.py:17
  1027.0 37.6 %collective-permute-start.1 = (f32[2,1024,128]{2,1,0:T(8,128)}, f32[2,1024,128]{2,1,0:T(8,128)}, u32[]{:S(2)}, u32[]{:S(2)}) collective-permute-start(f32[2,1024,128]{2,1,0:T(8,128)} %maximum_add_fusion.4), channel_id=1, source_target_pairs={{0,1},{1,2},{2,3},{3,4},{4,5},{5,6},{6,7},{7,8},{8,9},{9,10},{10,1... | collective-permute-start | bytes 3145736 | tf_op jit(solution)/shard_map/while/body/eval_jaxpr/ppermute | solution.py:17
  1027.0 37.6 %collective-permute-start = (bf16[2,1024,128]{2,1,0:T(8,128)(2,1)S(1)}, bf16[2,1024,128]{2,1,0:T(8,128)(2,1)}, u32[]{:S(2)}, u32[]{:S(2)}) collective-permute-start(bf16[2,1024,128]{2,1,0:T(8,128)(2,1)S(1)} %copy.139), channel_id=1, source_target_pairs={{0,1},{1,2},{2,3},{3,4},{4,5},{5,6},{6,7},{7,8},{8,9},{9,10},{10,1... | collective-permute-start | bytes 1572872 | tf_op jit(solution)/shard_map/while/body/eval_jaxpr/ppermute | solution.py:17
  1093.3 36.6 %collective-permute-start.1 = (f32[2,1024,128]{2,1,0:T(8,128)}, f32[2,1024,128]{2,1,0:T(8,128)}, u32[]{:S(2)}, u32[]{:S(2)}) collective-permute-start(f32[2,1024,128]{2,1,0:T(8,128)} %maximum_add_fusion.4), channel_id=1, source_target_pairs={{0,1},{1,2},{2,3},{3,4},{4,5},{5,6},{6,7},{7,8},{8,9},{9,10},{10,1... | collective-permute-start | bytes 3145736 | tf_op jit(solution)/shard_map/while/body/eval_jaxpr/ppermute | solution.py:17
  1093.3 36.6 %collective-permute-start = (bf16[2,1024,128]{2,1,0:T(8,128)(2,1)S(1)}, bf16[2,1024,128]{2,1,0:T(8,128)(2,1)}, u32[]{:S(2)}, u32[]{:S(2)}) collective-permute-start(bf16[2,1024,128]{2,1,0:T(8,128)(2,1)S(1)} %copy.139), channel_id=1, source_target_pairs={{0,1},{1,2},{2,3},{3,4},{4,5},{5,6},{6,7},{7,8},{8,9},{9,10},{10,1... | collective-permute-start | bytes 1572872 | tf_op jit(solution)/shard_map/while/body/eval_jaxpr/ppermute | solution.py:17
  1221.3 35.1 %collective-permute-start.1 = (f32[2,1024,128]{2,1,0:T(8,128)}, f32[2,1024,128]{2,1,0:T(8,128)}, u32[]{:S(2)}, u32[]{:S(2)}) collective-permute-start(f32[2,1024,128]{2,1,0:T(8,128)} %maximum_add_fusion.4), channel_id=1, source_target_pairs={{0,1},{1,2},{2,3},{3,4},{4,5},{5,6},{6,7},{7,8},{8,9},{9,10},{10,1... | collective-permute-start | bytes 3145736 | tf_op jit(solution)/shard_map/while/body/eval_jaxpr/ppermute | solution.py:17
  1221.3 35.1 %collective-permute-start = (bf16[2,1024,128]{2,1,0:T(8,128)(2,1)S(1)}, bf16[2,1024,128]{2,1,0:T(8,128)(2,1)}, u32[]{:S(2)}, u32[]{:S(2)}) collective-permute-start(bf16[2,1024,128]{2,1,0:T(8,128)(2,1)S(1)} %copy.139), channel_id=1, source_target_pairs={{0,1},{1,2},{2,3},{3,4},{4,5},{5,6},{6,7},{7,8},{8,9},{9,10},{10,1... | collective-permute-start | bytes 1572872 | tf_op jit(solution)/shard_map/while/body/eval_jaxpr/ppermute | solution.py:17
  1285.1 35.7 %collective-permute-start.1 = (f32[2,1024,128]{2,1,0:T(8,128)}, f32[2,1024,128]{2,1,0:T(8,128)}, u32[]{:S(2)}, u32[]{:S(2)}) collective-permute-start(f32[2,1024,128]{2,1,0:T(8,128)} %maximum_add_fusion.4), channel_id=1, source_target_pairs={{0,1},{1,2},{2,3},{3,4},{4,5},{5,6},{6,7},{7,8},{8,9},{9,10},{10,1... | collective-permute-start | bytes 3145736 | tf_op jit(solution)/shard_map/while/body/eval_jaxpr/ppermute | solution.py:17
  1285.1 35.7 %collective-permute-start = (bf16[2,1024,128]{2,1,0:T(8,128)(2,1)S(1)}, bf16[2,1024,128]{2,1,0:T(8,128)(2,1)}, u32[]{:S(2)}, u32[]{:S(2)}) collective-permute-start(bf16[2,1024,128]{2,1,0:T(8,128)(2,1)S(1)} %copy.139), channel_id=1, source_target_pairs={{0,1},{1,2},{2,3},{3,4},{4,5},{5,6},{6,7},{7,8},{8,9},{9,10},{10,1... | collective-permute-start | bytes 1572872 | tf_op jit(solution)/shard_map/while/body/eval_jaxpr/ppermute | solution.py:17
  1349.5 35.3 %collective-permute-start.1 = (f32[2,1024,128]{2,1,0:T(8,128)}, f32[2,1024,128]{2,1,0:T(8,128)}, u32[]{:S(2)}, u32[]{:S(2)}) collective-permute-start(f32[2,1024,128]{2,1,0:T(8,128)} %maximum_add_fusion.4), channel_id=1, source_target_pairs={{0,1},{1,2},{2,3},{3,4},{4,5},{5,6},{6,7},{7,8},{8,9},{9,10},{10,1... | collective-permute-start | bytes 3145736 | tf_op jit(solution)/shard_map/while/body/eval_jaxpr/ppermute | solution.py:17
  1349.5 35.3 %collective-permute-start = (bf16[2,1024,128]{2,1,0:T(8,128)(2,1)S(1)}, bf16[2,1024,128]{2,1,0:T(8,128)(2,1)}, u32[]{:S(2)}, u32[]{:S(2)}) collective-permute-start(bf16[2,1024,128]{2,1,0:T(8,128)(2,1)S(1)} %copy.139), channel_id=1, source_target_pairs={{0,1},{1,2},{2,3},{3,4},{4,5},{5,6},{6,7},{7,8},{8,9},{9,10},{10,1... | collective-permute-start | bytes 1572872 | tf_op jit(solution)/shard_map/while/body/eval_jaxpr/ppermute | solution.py:17
  1411.8 37.7 %collective-permute-start.1 = (f32[2,1024,128]{2,1,0:T(8,128)}, f32[2,1024,128]{2,1,0:T(8,128)}, u32[]{:S(2)}, u32[]{:S(2)}) collective-permute-start(f32[2,1024,128]{2,1,0:T(8,128)} %maximum_add_fusion.4), channel_id=1, source_target_pairs={{0,1},{1,2},{2,3},{3,4},{4,5},{5,6},{6,7},{7,8},{8,9},{9,10},{10,1... | collective-permute-start | bytes 3145736 | tf_op jit(solution)/shard_map/while/body/eval_jaxpr/ppermute | solution.py:17
  1411.8 37.6 %collective-permute-start = (bf16[2,1024,128]{2,1,0:T(8,128)(2,1)S(1)}, bf16[2,1024,128]{2,1,0:T(8,128)(2,1)}, u32[]{:S(2)}, u32[]{:S(2)}) collective-permute-start(bf16[2,1024,128]{2,1,0:T(8,128)(2,1)S(1)} %copy.139), channel_id=1, source_target_pairs={{0,1},{1,2},{2,3},{3,4},{4,5},{5,6},{6,7},{7,8},{8,9},{9,10},{10,1... | collective-permute-start | bytes 1572872 | tf_op jit(solution)/shard_map/while/body/eval_jaxpr/ppermute | solution.py:17
  1478.2 36.7 %collective-permute-start.1 = (f32[2,1024,128]{2,1,0:T(8,128)}, f32[2,1024,128]{2,1,0:T(8,128)}, u32[]{:S(2)}, u32[]{:S(2)}) collective-permute-start(f32[2,1024,128]{2,1,0:T(8,128)} %maximum_add_fusion.4), channel_id=1, source_target_pairs={{0,1},{1,2},{2,3},{3,4},{4,5},{5,6},{6,7},{7,8},{8,9},{9,10},{10,1... | collective-permute-start | bytes 3145736 | tf_op jit(solution)/shard_map/while/body/eval_jaxpr/ppermute | solution.py:17
  1478.2 36.7 %collective-permute-start = (bf16[2,1024,128]{2,1,0:T(8,128)(2,1)S(1)}, bf16[2,1024,128]{2,1,0:T(8,128)(2,1)}, u32[]{:S(2)}, u32[]{:S(2)}) collective-permute-start(bf16[2,1024,128]{2,1,0:T(8,128)(2,1)S(1)} %copy.139), channel_id=1, source_target_pairs={{0,1},{1,2},{2,3},{3,4},{4,5},{5,6},{6,7},{7,8},{8,9},{9,10},{10,1... | collective-permute-start | bytes 1572872 | tf_op jit(solution)/shard_map/while/body/eval_jaxpr/ppermute | solution.py:17
  1543.6 34.1 %collective-permute-start.1 = (f32[2,1024,128]{2,1,0:T(8,128)}, f32[2,1024,128]{2,1,0:T(8,128)}, u32[]{:S(2)}, u32[]{:S(2)}) collective-permute-start(f32[2,1024,128]{2,1,0:T(8,128)} %maximum_add_fusion.4), channel_id=1, source_target_pairs={{0,1},{1,2},{2,3},{3,4},{4,5},{5,6},{6,7},{7,8},{8,9},{9,10},{10,1... | collective-permute-start | bytes 3145736 | tf_op jit(solution)/shard_map/while/body/eval_jaxpr/ppermute | solution.py:17
  1543.6 34.1 %collective-permute-start = (bf16[2,1024,128]{2,1,0:T(8,128)(2,1)S(1)}, bf16[2,1024,128]{2,1,0:T(8,128)(2,1)}, u32[]{:S(2)}, u32[]{:S(2)}) collective-permute-start(bf16[2,1024,128]{2,1,0:T(8,128)(2,1)S(1)} %copy.139), channel_id=1, source_target_pairs={{0,1},{1,2},{2,3},{3,4},{4,5},{5,6},{6,7},{7,8},{8,9},{9,10},{10,1... | collective-permute-start | bytes 1572872 | tf_op jit(solution)/shard_map/while/body/eval_jaxpr/ppermute | solution.py:17
  (275 other events, 4097.1 us)
Sparse Core Ops, SparseCore 0:
  22.1 51.8 all-gather.2
where the time goes:
time: 1640 us; the launch traced here: 1630 us
  waiting for transfers between devices  529 us (32%)
  blocking collectives  260 us (16%)
  other arithmetic  221 us (13%)
  matrix products  191 us (12%)
  loops' own time  176 us (11%)
  local copies, waits for them, and re-layouts  123 us (8%)
  starting transfers between devices  115 us (7%)
    ppermute x32, waiting for transfers between devices, shifted(): return lax.ppermute(value, axis, pairs)  508 us
    all_gather x1, blocking collectives, local(): lax.all_gather(positions, ('head', 'inner', 'outer'), axis=0, tiled=True)  232 us
    another operation x1, loops' own time, local(): lax.fori_loop(0, cycle_count, cycle_step, (kv_start, start_grads, start_q...  87.2 us
    another operation x1, loops' own time, local(): lax.fori_loop(0, piece_rows // key_span, one_tile, jnp.zeros((QH_DEV, ctx...  84.8 us
    all_to_all x1, starting transfers between devices, local(): lax.all_to_all(grad_output, 'head', split_axis=1, concat_axis=0, tiled=True)  84 us
    dot_general x33, matrix products, active_tile(): jnp.einsum('qed,kd->eqk', dout_tile, value_tile, preferred_element_type=j...  67.6 us
    dot_general x33, matrix products, active_tile(): jnp.einsum('eqk,qed->kd', weights_low, dout_tile, preferred_element_type=...  50.9 us
    reduce_min x32, other arithmetic, tile_sums(): jnp.min(key_pos) <= jnp.max(query_pos)  44.4 us
  transfers between devices with their start and end apart: 39, of which 20 were waited for; matrix products, arithmetic and copies ran while one was open for 10% of the time, Pallas kernels for 0%

commit v1 on v0

v1 whole, which is shorter than its diff:
```python
import functools, math
import jax, jax.numpy as jnp
from jax import lax
from jax.experimental import pallas as pl
from jax.experimental.pallas import tpu as pltpu
from jax.sharding import PartitionSpec as P

f32, bf16 = jnp.float32, jnp.bfloat16
HD = 128
TILE = 512
SCALE = 1.0 / 600.0
CAP2 = 50.0 * math.log2(math.e)

def nt(a, b):
    return lax.dot_general(a, b, (((1,), (1,)), ((), ())), preferred_element_type=f32)

def nn(a, b):
    return lax.dot_general(a, b, (((1,), (0,)), ((), ())), preferred_element_type=f32)

def totals_kernel(nr, nk, span_ref, q_ref, k_ref, qpos_ref, kpos_ref, z_ref):
    z_ref[...] = jnp.zeros_like(z_ref)

    def tile(rb, kb, masked):
        rows = pl.ds(pl.multiple_of(rb * TILE, TILE), TILE)
        kk = k_ref[pl.ds(pl.multiple_of(kb * TILE, TILE), TILE), :]
        if masked:
            live = kpos_ref[pl.ds(pl.multiple_of(kb * TILE, TILE), TILE), :] <= qpos_ref[rb]
        for h in range(2):
            s = nt(kk, q_ref[rows, h * HD:(h + 1) * HD])
            e = jnp.exp2(jnp.tanh(s * SCALE) * CAP2)
            if masked:
                e = jnp.where(live, e, 0.0)
            z_ref[rb, h] += jnp.sum(e.reshape(TILE // 8, 8, TILE), axis=0)

    def step(i, _):
        rb, kb = i // nk, i % nk
        some = span_ref[2, kb] <= span_ref[1, rb]
        whole = span_ref[3, kb] <= span_ref[0, rb]
        pl.when(whole)(lambda: tile(rb, kb, False))
        pl.when(jnp.logical_and(some, jnp.logical_not(whole)))(lambda: tile(rb, kb, True))
        return 0

    lax.fori_loop(0, nr * nk, step, 0)

def totals(span, q, k, qpos, kpos):
    nr, nk = q.shape[0] // TILE, k.shape[0] // TILE
    vm = pl.BlockSpec(memory_space=pltpu.VMEM)
    return pl.pallas_call(
        functools.partial(totals_kernel, nr, nk),
        out_shape=jax.ShapeDtypeStruct((nr, 2, 8, TILE), f32),
        in_specs=[pl.BlockSpec(memory_space=pltpu.SMEM), vm, vm, vm, vm],
        out_specs=vm,
        compiler_params=pltpu.CompilerParams(vmem_limit_bytes=56 * 2**20),
        cost_estimate=pl.CostEstimate(flops=10**10, bytes_accessed=4 * 2**20, transcendentals=3 * 10**7),
        name="totals",
    )(span, q, k, qpos.reshape(nr, 1, TILE), kpos.reshape(-1, 1))

def grads_kernel(nr, nk, span_ref, q_ref, do_ref, k_ref, v_ref, z_ref, d_ref, qpos_ref, kpos_ref,
                 dq_ref, dk_ref, dv_ref, qt, dot, dq, dkt, dvt, lcol, dcol):
    dq[...] = jnp.zeros_like(dq)
    dkt[...] = jnp.zeros_like(dkt)
    dvt[...] = jnp.zeros_like(dvt)

    def prep(rb, _):
        rows = pl.ds(pl.multiple_of(rb * TILE, TILE), TILE)
        for h in range(2):
            cols = slice(h * HD, (h + 1) * HD)
            qt[rb, h] = q_ref[rows, cols].T
            dot[rb, h] = do_ref[rows, cols].T
            lz = jnp.log2(z_ref[rb, h:h + 1, :])
            lcol[rb, h] = jnp.broadcast_to(lz, (HD, TILE)).T
            dcol[rb, h] = jnp.broadcast_to(d_ref[rb, h:h + 1, :], (HD, TILE)).T
        return 0

    lax.fori_loop(0, nr, prep, 0)

    def tile(rb, kb, masked):
        rows = pl.ds(pl.multiple_of(rb * TILE, TILE), TILE)
        keys = pl.ds(pl.multiple_of(kb * TILE, TILE), TILE)
        kk = k_ref[keys, :]
        vv = v_ref[keys, :]
        if masked:
            live = kpos_ref[kb] <= qpos_ref[rows, :]
        for h in range(2):
            cols = slice(h * HD, (h + 1) * HD)
            s = nt(q_ref[rows, cols], kk)
            dp = nt(do_ref[rows, cols], vv)
            lc = jnp.concatenate([lcol[rb, h]] * (TILE // HD), axis=1)
            dc = jnp.concatenate([dcol[rb, h]] * (TILE // HD), axis=1)
            t = jnp.tanh(s * SCALE)
            w = jnp.exp2(t * CAP2 - lc)
            if masked:
                w = jnp.where(live, w, 0.0)
            g = w * (dp - dc) * (1.0 - t * t)
            wl = w.astype(bf16)
            gl = g.astype(bf16)
            dvt[kb] += nn(dot[rb, h], wl)
            dkt[kb] += nn(qt[rb, h], gl)
            dq[rb, h] += nn(gl, kk)

    def step(i, _):
        rb, kb = i // nk, i % nk
        some = span_ref[2, kb] <= span_ref[1, rb]
        whole = span_ref[3, kb] <= span_ref[0, rb]
        pl.when(whole)(lambda: tile(rb, kb, False))
        pl.when(jnp.logical_and(some, jnp.logical_not(whole)))(lambda: tile(rb, kb, True))
        return 0

    lax.fori_loop(0, nr * nk, step, 0)

    def out_rows(rb, _):
        rows = pl.ds(pl.multiple_of(rb * TILE, TILE), TILE)
        for h in range(2):
            dq_ref[rows, h * HD:(h + 1) * HD] = (dq[rb, h] * (1.0 / 12.0)).astype(bf16)
        return 0

    def out_keys(kb, _):
        keys = pl.ds(pl.multiple_of(kb * TILE, TILE), TILE)
        dk_ref[keys, :] = (dkt[kb] * (1.0 / 12.0)).T.astype(bf16)
        dv_ref[keys, :] = dvt[kb].T.astype(bf16)
        return 0

    lax.fori_loop(0, nr, out_rows, 0)
    lax.fori_loop(0, nk, out_keys, 0)

def grads(span, q, do, k, v, z, d, qpos, kpos):
    nr, nk = q.shape[0] // TILE, k.shape[0] // TILE
    vm = pl.BlockSpec(memory_space=pltpu.VMEM)
    return pl.pallas_call(
        functools.partial(grads_kernel, nr, nk),
        out_shape=(jax.ShapeDtypeStruct(q.shape, bf16), jax.ShapeDtypeStruct(k.shape, bf16), jax.ShapeDtypeStruct(k.shape, bf16)),
        in_specs=[pl.BlockSpec(memory_space=pltpu.SMEM)] + [vm] * 8,
        out_specs=(vm,) * 3,
        scratch_shapes=[
            pltpu.VMEM((nr, 2, HD, TILE), bf16), pltpu.VMEM((nr, 2, HD, TILE), bf16),
            pltpu.VMEM((nr, 2, TILE, HD), f32),
            pltpu.VMEM((nk, HD, TILE), f32), pltpu.VMEM((nk, HD, TILE), f32),
            pltpu.VMEM((nr, 2, TILE, HD), f32), pltpu.VMEM((nr, 2, TILE, HD), f32),
        ],
        compiler_params=pltpu.CompilerParams(vmem_limit_bytes=56 * 2**20),
        cost_estimate=pl.CostEstimate(flops=5 * 10**10, bytes_accessed=16 * 2**20, transcendentals=3 * 10**7),
        name="grads",
    )(span, q, do, k, v, z, d, qpos.reshape(-1, 1), kpos.reshape(nk, 1, TILE))

def spans(qpos, kpos):
    qb, kb = qpos.reshape(-1, TILE), kpos.reshape(-1, TILE)
    return jnp.stack([qb.min(1), qb.max(1), kb.min(1), kb.max(1)])


MESH = pl.DeviceIdType.MESH
HEADS, INNER, OUTER, BLK, CTX_ROWS = 8, 4, 4, 128, 1024


def peers():
    head, inner, outer = (lax.axis_index(a) for a in ("head", "inner", "outer"))
    y_peer = lax.rem(inner + 2, INNER)
    core_peer = inner + 1 - 2 * lax.rem(inner, 2)
    x_next, x_prev = lax.rem(outer + 1, OUTER), lax.rem(outer + OUTER - 1, OUTER)
    return head, inner, outer, y_peer, core_peer, x_next, x_prev


def greet(devices):
    barrier = pltpu.get_barrier_semaphore()
    for device in devices:
        pl.semaphore_signal(barrier, inc=1, device_id=device, device_id_type=MESH)
    pl.semaphore_wait(barrier, len(devices))


def rows_at(ref, block, chunk):
    return ref.at[pl.ds(pl.multiple_of(block * CTX_ROWS + chunk * BLK, BLK), BLK)]


def spread_kernel(q, do, k, v, aux, q_all, do_all, k_all, v_all, aux_r, aux_k,
                  send1, recv1, send2, recv2, own_sem):
    head, inner, outer, y_peer, core_peer, x_next, x_prev = peers()
    greet([{"head": lax.rem(head + j, HEADS)} for j in range(1, HEADS)]
          + [{"inner": y_peer}, {"inner": core_peer}, {"outer": x_next}, {"outer": x_prev}])

    def aux_at(ref, block, chunk):
        return ref.at[block, chunk]

    def first(t, dest, source_head):
        if t == 4:
            return aux.at[dest], aux_at(aux_r, inner, source_head)
        src = (q, do, k, v)[t]
        dst = (q_all, do_all, k_all, v_all)[t]
        wide = 256 if t < 2 else 128
        return (src.at[:, pl.ds(pl.multiple_of(dest * wide, wide), wide)],
                rows_at(dst, inner if t < 2 else outer, source_head))

    def remote(src, dst, ssem, rsem, device):
        return pltpu.make_async_remote_copy(src_ref=src, dst_ref=dst, send_sem=ssem, recv_sem=rsem,
                                            device_id=device, device_id_type=MESH)

    ORDER = (0, 2, 4, 3, 1)
    for t in ORDER:
        src, dst = first(t, head, head)
        pltpu.make_async_copy(src, dst, own_sem.at[t]).start()

    def send_first(j, _):
        dest = lax.rem(head + j, HEADS)
        for t in ORDER:
            src, dst = first(t, dest, head)
            remote(src, dst, send1.at[t, dest], recv1.at[t, head], {"head": dest}).start()
        return 0

    lax.fori_loop(1, HEADS, send_first, 0)
    for t in ORDER:
        src, dst = first(t, head, head)
        pltpu.make_async_copy(src, dst, own_sem.at[t]).wait()

    def piece(t, block, chunk):
        if t == 4:
            return aux_at(aux_r, block, chunk)
        if t == 5:
            return aux_at(aux_k, block, chunk)
        return rows_at((q_all, do_all, k_all, v_all)[t], block, chunk)

    ROWS, KEYS = (0, 4, 1), (2, 5, 3)

    def hop(route, t, block, chunk, device):
        ref = piece(t, block, chunk)
        s = (ROWS if t in ROWS else KEYS).index(t)
        return remote(ref, ref, send2.at[route, s, chunk], recv2.at[route, s, chunk], device)

    def aux_hop(route, chunk, device):
        return remote(aux_at(aux_r, inner, chunk), aux_at(aux_k, outer, chunk),
                      send2.at[route, 1, chunk], recv2.at[route, 1, chunk], device)

    Y, C, XN, XP = {"inner": y_peer}, {"inner": core_peer}, {"outer": x_next}, {"outer": x_prev}

    def forward(j, _):
        chunk = lax.rem(head + HEADS - j, HEADS)

        @pl.when(j > 0)
        def _():
            for t in ORDER:
                src, dst = first(t, head, chunk)
                remote(src, dst, send1.at[t, chunk], recv1.at[t, chunk], {"head": chunk}).wait_recv()

        own = pltpu.make_async_copy(aux_at(aux_r, inner, chunk), aux_at(aux_k, outer, chunk), own_sem.at[5])
        own.start()
        for t in ROWS:
            hop(0, t, inner, chunk, Y).start()
            hop(1, t, inner, chunk, C).start()
        for t in KEYS:
            if t == 5:
                aux_hop(3, chunk, XN).start()
                aux_hop(4, chunk, XP).start()
            else:
                hop(3, t, outer, chunk, XN).start()
                hop(4, t, outer, chunk, XP).start()
        own.wait()
        return 0

    lax.fori_loop(0, HEADS, forward, 0)

    def relay(j, _):
        chunk = lax.rem(head + HEADS - j, HEADS)
        for t in ROWS:
            hop(0, t, y_peer, chunk, Y).wait_recv()
            hop(2, t, y_peer, chunk, C).start()
        even = lax.rem(chunk, 2) == 0
        for t in KEYS:
            hop(3, t, x_prev, chunk, XN).wait_recv()

            @pl.when(even)
            def _():
                hop(5, t, x_prev, chunk, XN).start()

            hop(4, t, x_next, chunk, XP).wait_recv()

            @pl.when(jnp.logical_not(even))
            def _():
                hop(5, t, x_next, chunk, XP).start()
        return 0

    lax.fori_loop(0, HEADS, relay, 0)
    y_core = lax.rem(core_peer + 2, INNER)
    x_far = lax.rem(outer + 2, OUTER)

    def finish(j, _):
        chunk = lax.rem(head + HEADS - j, HEADS)
        for t in ROWS:
            hop(1, t, core_peer, chunk, C).wait_recv()
            hop(2, t, y_core, chunk, C).wait_recv()
            hop(0, t, inner, chunk, Y).wait_send()
            hop(1, t, inner, chunk, C).wait_send()
            hop(2, t, y_peer, chunk, C).wait_send()
        for t in KEYS:
            hop(5, t, x_far, chunk, XN).wait_recv()
            hop(3, t, outer, chunk, XN).wait_send()
            hop(4, t, outer, chunk, XP).wait_send()
            hop(5, t, x_prev, chunk, XN).wait_send()

        @pl.when(j > 0)
        def _():
            for t in ORDER:
                src, dst = first(t, chunk, head)
                remote(src, dst, send1.at[t, chunk], recv1.at[t, chunk], {"head": chunk}).wait_send()
        return 0

    lax.fori_loop(0, HEADS, finish, 0)


def spread(q, do, k, v, aux):
    hbm = pl.BlockSpec(memory_space=pl.ANY)
    rows = INNER * CTX_ROWS
    return pl.pallas_call(
        spread_kernel,
        out_shape=(jax.ShapeDtypeStruct((rows, 256), bf16), jax.ShapeDtypeStruct((rows, 256), bf16),
                   jax.ShapeDtypeStruct((rows, 128), bf16), jax.ShapeDtypeStruct((rows, 128), bf16),
                   jax.ShapeDtypeStruct((INNER, HEADS, 8, 128), f32), jax.ShapeDtypeStruct((OUTER, HEADS, 8, 128), f32)),
        in_specs=[hbm] * 5,
        out_specs=(hbm,) * 6,
        scratch_shapes=[pltpu.SemaphoreType.DMA((5, HEADS)), pltpu.SemaphoreType.DMA((5, HEADS)),
                        pltpu.SemaphoreType.DMA((6, 3, HEADS)), pltpu.SemaphoreType.DMA((6, 3, HEADS)),
                        pltpu.SemaphoreType.DMA((6,))],
        compiler_params=pltpu.CompilerParams(collective_id=0, has_side_effects=True),
        name="spread",
    )(q, do, k, v, aux)


def pool_kernel(z, out, recv, send_sem, recv_sem):
    head, inner, outer, y_peer, core_peer, x_next, x_prev = peers()
    others = [lax.rem(inner + j, INNER) for j in range(1, INNER)]
    greet([{"inner": o} for o in others])
    out[...] = jnp.sum(z[...], axis=2)
    copies = []
    for j, o in enumerate(others):
        copies.append(pltpu.make_async_remote_copy(
            src_ref=out, dst_ref=recv.at[j], send_sem=send_sem.at[j], recv_sem=recv_sem.at[j],
            device_id={"inner": o}, device_id_type=MESH))
        copies[-1].start()
    for c in copies:
        c.wait()
    total = jnp.zeros(out.shape, f32)
    for i in range(INNER):
        d = lax.rem(inner - i + INNER, INNER)
        part = jnp.where(d == 0, out[...], jnp.where(d == 1, recv[0], jnp.where(d == 2, recv[1], recv[2])))
        total = total + part
    out[...] = total


def pool(z):
    vm = pl.BlockSpec(memory_space=pltpu.VMEM)
    small = (z.shape[0], 2, z.shape[3])
    return pl.pallas_call(
        pool_kernel,
        out_shape=jax.ShapeDtypeStruct(small, f32),
        in_specs=[vm], out_specs=vm,
        scratch_shapes=[pltpu.VMEM((3,) + small, f32), pltpu.SemaphoreType.DMA((3,)), pltpu.SemaphoreType.DMA((3,))],
        compiler_params=pltpu.CompilerParams(collective_id=1, has_side_effects=True),
        name="pool",
    )(z)


def collect_kernel(dq, dk, dv, gq, gk, gv, dq_pair, dq_sum, dq_far, kv_far, low_q, low_k, low_v,
                   send_sem, recv_sem, send_out, recv_out, own_sem):
    head, inner, outer, y_peer, core_peer, x_next, x_prev = peers()
    x_far = lax.rem(outer + 2, OUTER)
    greet([{"head": lax.rem(head + j, HEADS)} for j in range(1, HEADS)]
          + [{"inner": y_peer}, {"inner": core_peer}, {"outer": x_next}, {"outer": x_prev}, {"outer": x_far}])
    y_core = lax.rem(core_peer + 2, INNER)
    Y, C = {"inner": y_peer}, {"inner": core_peer}
    XS = ({"outer": x_next}, {"outer": x_far}, {"outer": x_prev})
    XI = (x_next, x_far, x_prev)

    def remote(src, dst, ssem, rsem, device):
        return pltpu.make_async_remote_copy(src_ref=src, dst_ref=dst, send_sem=ssem, recv_sem=rsem,
                                            device_id=device, device_id_type=MESH)

    def local_rows(chunk):
        return pl.ds(pl.multiple_of(chunk * BLK, BLK), BLK)

    def pair_copy(which, chunk):
        block = core_peer if which == 0 else y_core
        return remote(rows_at(dq, block, chunk), dq_pair.at[which, local_rows(chunk)],
                      send_sem.at[which, chunk], recv_sem.at[which, chunk], C)

    def far_copy(chunk):
        return remote(dq_sum.at[local_rows(chunk)], dq_far.at[local_rows(chunk)],
                      send_sem.at[2, chunk], recv_sem.at[2, chunk], Y)

    def kv_copy(t, x, chunk):
        n = 3 + 3 * t + x
        return remote(rows_at((dk, dv)[t], XI[x], chunk), kv_far.at[t, x, local_rows(chunk)],
                      send_sem.at[n, chunk], recv_sem.at[n, chunk], XS[x])

    def out_copy(t, chunk):
        low, out, wide = ((low_q, gq, 256), (low_k, gk, 128), (low_v, gv, 128))[t]
        return remote(low.at[local_rows(chunk)], out.at[:, pl.ds(pl.multiple_of(head * wide, wide), wide)],
                      send_out.at[t, chunk], recv_out.at[t, head], {"head": chunk})

    def chunk_at(j):
        return lax.rem(head + 1 + j, HEADS)

    def send_pair(j, _):
        chunk = chunk_at(j)
        pair_copy(0, chunk).start()
        pair_copy(1, chunk).start()
        for t in range(2):
            for x in range(3):
                kv_copy(t, x, chunk).start()
        return 0

    lax.fori_loop(0, HEADS, send_pair, 0)

    def block_rows(block, chunk):
        return pl.ds(pl.multiple_of(block * CTX_ROWS + chunk * BLK, BLK), BLK)

    def sum_pair(j, _):
        chunk = chunk_at(j)
        pair_copy(0, chunk).wait_recv()
        pair_copy(1, chunk).wait_recv()
        rows = local_rows(chunk)
        dq_sum[rows, :] = (dq[block_rows(y_peer, chunk), :].astype(f32) + dq_pair[1, rows, :].astype(f32)).astype(bf16)
        far_copy(chunk).start()
        return 0

    lax.fori_loop(0, HEADS, sum_pair, 0)

    def sum_all(j, _):
        chunk = chunk_at(j)
        rows = local_rows(chunk)
        for t in range(2):
            for x in range(3):
                kv_copy(t, x, chunk).wait_recv()
            src, low = ((dk, low_k), (dv, low_v))[t]
            total = src[block_rows(outer, chunk), :].astype(f32)
            for x in range(3):
                total = total + kv_far[t, x, rows, :].astype(f32)
            low[rows, :] = total.astype(bf16)
        far_copy(chunk).wait_recv()
        low_q[rows, :] = (dq[block_rows(inner, chunk), :].astype(f32) + dq_pair[0, rows, :].astype(f32)
                          + dq_far[rows, :].astype(f32)).astype(bf16)

        @pl.when(j < HEADS - 1)
        def _():
            for t in range(3):
                out_copy(t, chunk).start()
        return 0

    lax.fori_loop(0, HEADS, sum_all, 0)
    own = []
    for t in range(3):
        low, out, wide = ((low_q, gq, 256), (low_k, gk, 128), (low_v, gv, 128))[t]
        own.append(pltpu.make_async_copy(low.at[local_rows(head)],
                                         out.at[:, pl.ds(pl.multiple_of(head * wide, wide), wide)], own_sem.at[t]))
        own[-1].start()

    def finish(j, _):
        chunk = chunk_at(j)
        for which in range(2):
            pair_copy(which, chunk).wait_send()
        far_copy(chunk).wait_send()
        for t in range(2):
            for x in range(3):
                kv_copy(t, x, chunk).wait_send()

        @pl.when(j < HEADS - 1)
        def _():
            for t in range(3):
                low, out, wide = ((low_q, gq, 256), (low_k, gk, 128), (low_v, gv, 128))[t]
                out_copy(t, chunk).wait_send()
                remote(low.at[local_rows(head)], out.at[:, pl.ds(pl.multiple_of(chunk * wide, wide), wide)],
                       send_out.at[t, head], recv_out.at[t, chunk], {"head": chunk}).wait_recv()
        return 0

    lax.fori_loop(0, HEADS, finish, 0)
    for copy in own:
        copy.wait()


def collect(dq, dk, dv):
    vm = pl.BlockSpec(memory_space=pltpu.VMEM)
    hbm = pl.BlockSpec(memory_space=pl.ANY)
    return pl.pallas_call(
        collect_kernel,
        out_shape=(jax.ShapeDtypeStruct((BLK, 2048), bf16), jax.ShapeDtypeStruct((BLK, 1024), bf16),
                   jax.ShapeDtypeStruct((BLK, 1024), bf16)),
        in_specs=[vm] * 3,
        out_specs=(hbm,) * 3,
        scratch_shapes=[pltpu.VMEM((2, CTX_ROWS, 256), bf16), pltpu.VMEM((CTX_ROWS, 256), bf16),
                        pltpu.VMEM((CTX_ROWS, 256), bf16), pltpu.VMEM((2, 3, CTX_ROWS, 128), bf16),
                        pltpu.VMEM((CTX_ROWS, 256), bf16), pltpu.VMEM((CTX_ROWS, 128), bf16),
                        pltpu.VMEM((CTX_ROWS, 128), bf16),
                        pltpu.SemaphoreType.DMA((9, HEADS)), pltpu.SemaphoreType.DMA((9, HEADS)),
                        pltpu.SemaphoreType.DMA((3, HEADS)), pltpu.SemaphoreType.DMA((3, HEADS)),
                        pltpu.SemaphoreType.DMA((3,))],
        compiler_params=pltpu.CompilerParams(collective_id=2, has_side_effects=True, vmem_limit_bytes=40 * 2**20),
        name="collect",
    )(dq, dk, dv)


def local(queries, keys, values, output, grad_output, positions):
    delta = jnp.sum((grad_output.astype(f32) * output.astype(f32)).reshape(BLK, HEADS, 2, HD), axis=3)
    delta = delta.transpose(1, 2, 0)
    place = jnp.broadcast_to(positions.astype(f32)[None, None, :], (HEADS, 1, BLK))
    aux = jnp.concatenate([delta, place, jnp.zeros((HEADS, 5, BLK), f32)], axis=1)
    q, do, k, v, aux_r, aux_k = spread(queries, grad_output, keys, values, aux)
    d = aux_r[:, :, 0:2, :].transpose(2, 0, 1, 3).reshape(2, -1, TILE).transpose(1, 0, 2)
    qpos = aux_r[:, :, 2, :].reshape(-1).astype(jnp.int32)
    kpos = aux_k[:, :, 2, :].reshape(-1).astype(jnp.int32)
    span = spans(qpos, kpos)
    z = pool(totals(span, q, k, qpos, kpos))
    dq, dk, dv = grads(span, q, do, k, v, z, d, qpos, kpos)
    return collect(dq, dk, dv)


def solution(mesh):
    rows = P(("head", "inner", "outer"), None)
    return jax.shard_map(
        local, mesh=mesh,
        in_specs=(rows,) * 5 + (P(("head", "inner", "outer")),),
        out_specs=(rows,) * 3,
        check_vma=False,
    )
```

time: 1640 us -> 227 us (0.14)
  waiting for transfers between devices: 529 us -> 0 us
  blocking collectives: 260 us -> 0 us
  other arithmetic: 221 us -> 9.27 us
  Pallas kernels: 0 us -> 202 us
  matrix products: 191 us -> 0 us
  loops' own time: 176 us -> 0 us
  starting transfers between devices: 115 us -> 0 us
  local copies, waits for them, and re-layouts: 123 us -> 13.2 us
    ppermute x32 -> x0, waiting for transfers between devices: 508 us -> none  [shifted(): return lax.ppermute(value, axis, pairs)]
    all_gather x1 -> x0, blocking collectives: 232 us -> none  [local(): lax.all_gather(positions, ('head', 'inner', 'outer'), axis=0, tiled=True)]
    pallas_call x0 -> x5, Pallas kernels: none -> 202 us  [the longest x1 75.4 us: grads(): pl.pallas_call(functools.partial(grads_kernel, nr, nk), out_shape=(jax.Sh...]
    dot_general x198 -> x0, matrix products: 191 us -> none  [the longest x33 67.6 us: active_tile(): jnp.einsum('qed,kd->eqk', dout_tile, value_tile, preferred_element_type=j...]
    another operation x130 -> x0, loops' own time: 176 us -> none  [the longest x1 87.2 us: local(): lax.fori_loop(0, cycle_count, cycle_step, (kv_start, start_grads, start_q...]
    add x128 -> x0, other arithmetic: 116 us -> none  [the longest x16 37.4 us: visit_block(): kv_grads + jnp.stack([jnp.concatenate(key_parts, axis=0), jnp.concatenate...]
    all_to_all x6 -> x0, starting transfers between devices: 113 us -> none  [the longest x1 84 us: local(): lax.all_to_all(grad_output, 'head', split_axis=1, concat_axis=0, tiled=True)]
    reduce_min x48 -> x3, other arithmetic: 54.6 us -> 3.58 us  [spans(): return jnp.stack([qb.min(1), qb.max(1), kb.min(1), kb.max(1)])]
  transfers between devices with their start and end apart: 39 -> 0, of which waited for: 20 -> 0; matrix products, arithmetic and copies ran while one was open for 10% -> 0% of each run, Pallas kernels for 0% -> 0%
where the time goes in v1:
time: 227 us; the launch traced here: 226 us
  Pallas kernels  202 us (89%)
  local copies, waits for them, and re-layouts  13.2 us (6%)
  other arithmetic  9.27 us (4%)
    pallas_call x1, Pallas kernels, grads(): pl.pallas_call(functools.partial(grads_kernel, nr, nk), out_shape=(jax.Sh...  75.4 us
    pallas_call x1, Pallas kernels, spread(): pl.pallas_call(spread_kernel, out_shape=(jax.ShapeDtypeStruct((rows, 256)...  53.8 us
    pallas_call x1, Pallas kernels, collect(): pl.pallas_call(collect_kernel, out_shape=(jax.ShapeDtypeStruct((BLK, 2048...  37.5 us
    pallas_call x1, Pallas kernels, totals(): pl.pallas_call(functools.partial(totals_kernel, nr, nk), out_shape=jax.Sh...  28.6 us
    pallas_call x1, Pallas kernels, pool(): pl.pallas_call(pool_kernel, out_shape=jax.ShapeDtypeStruct(small, f32), i...  7.15 us
    unnamed x13, local copies, waits for them, and re-layouts  6.25 us

profile of v1, /device:TPU:64, one launch (start us, length us, event | category | flops | bytes accessed | tf_op | source)
XLA Modules:
  0.0 225.6 jit_solution(6221126748507281221)
XLA Ops:
  0.6 0.7 convert_element_type.63
  1.4 1.3 convert_multiply_fusion
  2.7 0.9 reshape.71
  3.6 1.1 reduce_sum.9
  4.8 0.2 copy.11
  5.0 0.7 maximum_maximum_fusion.aux
  5.7 53.8 %spread.1 = (bf16[4096,256]{1,0:T(8,128)(2,1)}, bf16[4096,256]{1,0:T(8,128)(2,1)}, bf16[4096,128]{1,0:T(8,128)(2,1)}, bf16[4096,128]{1,0:T(8,128)(2,1)}, f32[4,8...) custom-call(bf16[128,2048]{1,0:T(8,128)(2,1)} %q.1, bf16[128,2048]{1,0:T(8,128)(2,1)} %do.1, bf16[128,1024]{1,0:T(8,128)(2,1)} %k.1, ...), custom_call_target="tpu_custom_call" | custom-call | tf_op jit(solution)/shard_map/spread/pallas_call | solution.py:309
  59.5 3.3 %fusion.1 = (s32[4,8]{1,0:T(4,128)S(1)}, s32[4,8]{1,0:T(4,128)S(1)}, s32[4,8]{1,0:T(4,128)S(1)}, s32[4,8]{1,0:T(4,128)S(1)}) fusion(f32[4,8,8,128]{3,2,1,0:T(8,128)} %get-tuple-element.12, f32[4,8,8,128]{3,2,1,0:T(8,128)} %get-tuple-element.13), kind=kLoop, calls=%fused_computation.6 | loop fusion | flops 24448 | bytes 33280 | tf_op jit(solution)/shard_map/reduce_min | solution.py:147
  62.8 1.0 slice_convert_fusion
  63.8 1.5 slice.11
  65.6 0.1 reduce_max.25
  66.2 0.6 pad_add_fusion.span_ref
  66.8 2.0 copy.13.qpos_ref
  68.7 2.0 copy.12.kpos_ref
  70.7 28.6 %totals.1.z = f32[8,2,8,512]{3,2,1,0:T(8,128)} custom-call(s32[4,8]{1,0:T(4,128)} %pad_add_fusion.span_ref, bf16[4096,256]{1,0:T(8,128)(2,1)} %get-tuple-element.14.q_ref, bf16[4096,128]{1,0:T(8,128)(2,1)} %get-tuple-element.16.k_ref, s32[8,1,512]{2,1,0:T(1,128)} %bitcast.17, s32[4096,1]{1,0:T(8,128)} %copy.12.kpos_ref), custom_call_target="tpu_custom_call" | custom-call | flops 10000000000 | bytes 4194304 | tf_op jit(solution)/shard_map/totals/pallas_call | solution.py:48
  99.3 7.1 %pool.1.z_ref = f32[8,2,512]{2,1,0:T(2,128)} custom-call(f32[8,2,8,512]{3,2,1,0:T(8,128)} %totals.1.z), custom_call_target="tpu_custom_call" | custom-call | tf_op jit(solution)/shard_map/pool/pallas_call | solution.py:348
  106.4 75.4 %grads.1 = (bf16[4096,256]{1,0:T(8,128)(2,1)}, bf16[4096,128]{1,0:T(8,128)(2,1)}, bf16[4096,128]{1,0:T(8,128)(2,1)}) custom-call(s32[4,8]{1,0:T(4,128)} %pad_add_fusion.span_ref, bf16[4096,256]{1,0:T(8,128)(2,1)} %get-tuple-element.14.q_ref, bf16[4096,256]{1,0:T(8,128)(2,1)} %get-tuple-element.15.do_ref, bf16[4096,128]{1,0:T(8,128)(2,1)} %get-tuple-element.16.k_ref, ...), custom_call_target="tpu_custom_call" | custom-call | flops 49999998976 | bytes 16777216 | tf_op jit(solution)/shard_map/grads/pallas_call | solution.py:129
  181.8 1.6 copy-done
  183.4 1.2 copy-done.1
  184.6 1.2 copy-done.2
  185.9 37.5 %collect.1 = (bf16[128,2048]{1,0:T(8,128)(2,1)S(1)}, bf16[128,1024]{1,0:T(8,128)(2,1)S(1)}, bf16[128,1024]{1,0:T(8,128)(2,1)S(1)}) custom-call(bf16[4096,256]{1,0:T(8,128)(2,1)S(1)} %copy-done, bf16[4096,128]{1,0:T(8,128)(2,1)S(1)} %copy-done.1, bf16[4096,128]{1,0:T(8,128)(2,1)S(1)} %copy-done.2), custom_call_target="tpu_custom_call" | custom-call | tf_op jit(solution)/shard_map/collect/pallas_call | solution.py:478
  223.4 0.8 copy.17
  224.2 0.7 copy.18
  224.9 0.7 copy.19
  (17 shorter events, 0.8 us)
Async XLA Ops:
  63.8 6.9 %copy-start.3 = (s32[4,8,1,128]{3,2,1,0:T(1,128)}, s32[4,8,1,128]{3,2,1,0:T(1,128)S(1)}, u32[]{:S(2)}) copy-start(s32[4,8,1,128]{3,2,1,0:T(1,128)S(1)} %get-tuple-element.27) | copy-start | bytes 49156
  63.8 6.9 %copy-start.4 = (s32[4,8,1,128]{3,2,1,0:T(1,128)}, s32[4,8,1,128]{3,2,1,0:T(1,128)S(1)}, u32[]{:S(2)}) copy-start(s32[4,8,1,128]{3,2,1,0:T(1,128)S(1)} %get-tuple-element.28) | copy-start | bytes 49156
  181.8 1.6 copy-start
  183.4 1.2 copy-start.1
  184.6 1.2 copy-start.2

commit v2 on v1

v2 whole, which is shorter than its diff:
```python
import functools, math
import jax, jax.numpy as jnp
from jax import lax
from jax.experimental import pallas as pl
from jax.experimental.pallas import tpu as pltpu
from jax.sharding import PartitionSpec as P

f32, bf16 = jnp.float32, jnp.bfloat16
HD = 128
TILE = 512
STRIP = 256
SCALE = 1.0 / 600.0
CAP2 = 50.0 * math.log2(math.e)

def nt(a, b):
    return lax.dot_general(a, b, (((1,), (1,)), ((), ())), preferred_element_type=f32)

def nn(a, b):
    return lax.dot_general(a, b, (((1,), (0,)), ((), ())), preferred_element_type=f32)

def place_of(aux, block):
    part = aux[block // 2, pl.ds(pl.multiple_of(lax.rem(block, 2) * 4, 4), 4), 2:3, :]
    return jnp.concatenate([part[c] for c in range(4)], axis=1)


def delta_of(aux, block, h):
    part = aux[block // 2, pl.ds(pl.multiple_of(lax.rem(block, 2) * 4, 4), 4), h:h + 1, :]
    return jnp.concatenate([part[c] for c in range(4)], axis=1)


def column(row):
    return jnp.broadcast_to(row, (HD, TILE)).T


def widen(col):
    return jnp.concatenate([col] * (TILE // HD), axis=1)


WHOLE, PARTLY = 0, 4096


def live_tiles(nr, nk, aux_r, aux_k, span, tiles):
    for b in range(nr):
        part = aux_r[b // 2, 4 * (b % 2):4 * (b % 2) + 4, 2, :]
        span[0, b] = jnp.min(part)
        span[1, b] = jnp.max(part)
    for b in range(nk):
        part = aux_k[b // 2, 4 * (b % 2):4 * (b % 2) + 4, 2, :]
        span[2, b] = jnp.min(part)
        span[3, b] = jnp.max(part)
    tiles[1] = nr * 64 + nk

    def scan(i, n):
        kb, rb = i // nr, lax.rem(i, nr)
        some = span[2, kb] <= span[1, rb]
        whole = span[3, kb] <= span[0, rb]

        @pl.when(some)
        def _():
            tiles[n + 2] = jnp.where(whole, WHOLE, PARTLY) + rb * 64 + kb
        return n + some.astype(jnp.int32)

    n = lax.fori_loop(0, nr * nk, scan, 0)
    tiles[0] = n
    tiles[n + 2] = nr * 64 + nk


def totals_kernel(nr, nk, q_ref, k_ref, aux_r, aux_k, z_ref, tiles, span):
    z_ref[...] = jnp.zeros_like(z_ref)
    live_tiles(nr, nk, aux_r, aux_k, span, tiles)

    def tile(rb, kb, masked):
        rows = pl.ds(pl.multiple_of(rb * TILE, TILE), TILE)
        kk = k_ref[pl.ds(pl.multiple_of(kb * TILE, TILE), TILE), :]
        if masked:
            live = widen(column(place_of(aux_k, kb))) <= place_of(aux_r, rb)
        for h in range(2):
            s = nt(kk, q_ref[rows, h * HD:(h + 1) * HD])
            e = jnp.exp2(jnp.tanh(s * SCALE) * CAP2)
            if masked:
                e = jnp.where(live, e, 0.0)
            z_ref[rb, h] += jnp.sum(e.reshape(TILE // 8, 8, TILE), axis=0)

    def step(i, _):
        code = tiles[i + 2]
        rb, kb = (code // 64) % 64, code % 64
        pl.when(code < PARTLY)(lambda: tile(rb, kb, False))
        pl.when(code >= PARTLY)(lambda: tile(rb, kb, True))
        return 0

    lax.fori_loop(0, tiles[0], step, 0)


def totals(q, k, aux_r, aux_k):
    nr, nk = q.shape[0] // TILE, k.shape[0] // TILE
    vm = pl.BlockSpec(memory_space=pltpu.VMEM)
    return pl.pallas_call(
        functools.partial(totals_kernel, nr, nk),
        out_shape=(jax.ShapeDtypeStruct((nr, 2, 8, TILE), f32), jax.ShapeDtypeStruct((nr * nk + 8,), jnp.int32)),
        in_specs=[vm, vm, vm, vm],
        out_specs=(vm, pl.BlockSpec(memory_space=pltpu.SMEM)),
        scratch_shapes=[pltpu.SMEM((4, 8), f32)],
        compiler_params=pltpu.CompilerParams(vmem_limit_bytes=60 * 2**20),
        cost_estimate=pl.CostEstimate(flops=2 * 10**10, bytes_accessed=4 * 2**20, transcendentals=3 * 10**7),
        name="totals",
    )(q, k, aux_r, aux_k)


def grads_kernel(nr, nk, tiles, q_ref, do_ref, k_ref, v_ref, z_ref, aux_r, aux_k,
                 dq_ref, dk_ref, dv_ref, qs, dos, qt, dot, dq, dkt, dvt, lcol, dcol, wbuf, gbuf):
    dq[...] = jnp.zeros_like(dq)
    dkt[...] = jnp.zeros_like(dkt)
    dvt[...] = jnp.zeros_like(dvt)

    def prep(rb, _):
        rows = pl.ds(pl.multiple_of(rb * TILE, TILE), TILE)
        for h in range(2):
            cols = slice(h * HD, (h + 1) * HD)
            hr = slice(h * TILE, (h + 1) * TILE)
            qs[rb, hr, :] = q_ref[rows, cols]
            dos[rb, hr, :] = do_ref[rows, cols]
            qt[rb, :, hr] = q_ref[rows, cols].T
            dot[rb, :, hr] = do_ref[rows, cols].T
            lcol[rb, hr, :] = column(jnp.log2(z_ref[rb, h:h + 1, :]))
            dcol[rb, hr, :] = column(delta_of(aux_r, rb, h))
        return 0

    lax.fori_loop(0, nr, prep, 0)

    def keys_of(ref, kb):
        return ref[pl.ds(pl.multiple_of(kb * TILE, TILE), TILE), :]

    def body(i, masked):
        now, last = tiles[i + 2], tiles[i + 1]
        rc, kc = (last // 64) % 64, last % 64
        ra, ka = jnp.minimum((now // 64) % 64, nr - 1), jnp.minimum(now % 64, nk - 1)
        kk = keys_of(k_ref, ka)
        vv = keys_of(v_ref, ka)
        kcc = keys_of(k_ref, jnp.minimum(kc, nk - 1))
        if masked:
            live = place_of(aux_k, ka) <= widen(column(place_of(aux_r, ra)))
        dv_sum, dk_sum = dvt[kc], dkt[kc]
        for c in range(2 * TILE // STRIP):
            hr = slice(c * STRIP, (c + 1) * STRIP)
            w, g = wbuf[hr, :], gbuf[hr, :]
            dv_sum = dv_sum + nn(dot[rc, :, hr], w)
            dk_sum = dk_sum + nn(qt[rc, :, hr], g)
            dq[rc, hr, :] += nn(g, kcc)
            t = jnp.tanh(nt(qs[ra, hr, :], kk) * SCALE)
            p = nt(dos[ra, hr, :], vv)
            w = jnp.exp2(t * CAP2 - widen(lcol[ra, hr, :]))
            if masked:
                lo = c * STRIP % TILE
                w = jnp.where(live[lo:lo + STRIP], w, 0.0)
            g = w * (p - widen(dcol[ra, hr, :])) * (1.0 - t * t)
            wbuf[hr, :] = w.astype(bf16)
            gbuf[hr, :] = g.astype(bf16)
        dvt[kc] = dv_sum
        dkt[kc] = dk_sum

    def step(i, _):
        masked = tiles[i + 2] >= PARTLY
        pl.when(jnp.logical_not(masked))(lambda: body(i, False))
        pl.when(masked)(lambda: body(i, True))
        return 0

    lax.fori_loop(0, tiles[0] + 1, step, 0)

    def out_rows(rb, _):
        rows = pl.ds(pl.multiple_of(rb * TILE, TILE), TILE)
        for h in range(2):
            dq_ref[rows, h * HD:(h + 1) * HD] = (dq[rb, h * TILE:(h + 1) * TILE, :] * (1.0 / 12.0)).astype(bf16)
        return 0

    def out_keys(kb, _):
        keys = pl.ds(pl.multiple_of(kb * TILE, TILE), TILE)
        dk_ref[keys, :] = (dkt[kb] * (1.0 / 12.0)).T.astype(bf16)
        dv_ref[keys, :] = dvt[kb].T.astype(bf16)
        return 0

    lax.fori_loop(0, nr, out_rows, 0)
    lax.fori_loop(0, nk, out_keys, 0)


def grads(tiles, q, do, k, v, z, aux_r, aux_k):
    nr, nk = q.shape[0] // TILE, k.shape[0] // TILE
    vm = pl.BlockSpec(memory_space=pltpu.VMEM)
    return pl.pallas_call(
        functools.partial(grads_kernel, nr, nk),
        out_shape=(jax.ShapeDtypeStruct(q.shape, bf16), jax.ShapeDtypeStruct(k.shape, bf16), jax.ShapeDtypeStruct(k.shape, bf16)),
        in_specs=[pl.BlockSpec(memory_space=pltpu.SMEM)] + [vm] * 7,
        out_specs=(vm,) * 3,
        scratch_shapes=[
            pltpu.VMEM((nr, 2 * TILE, HD), bf16), pltpu.VMEM((nr, 2 * TILE, HD), bf16),
            pltpu.VMEM((nr + 1, HD, 2 * TILE), bf16), pltpu.VMEM((nr + 1, HD, 2 * TILE), bf16),
            pltpu.VMEM((nr + 1, 2 * TILE, HD), f32),
            pltpu.VMEM((nk + 1, HD, TILE), f32), pltpu.VMEM((nk + 1, HD, TILE), f32),
            pltpu.VMEM((nr, 2 * TILE, HD), f32), pltpu.VMEM((nr, 2 * TILE, HD), f32),
            pltpu.VMEM((2 * TILE, TILE), bf16), pltpu.VMEM((2 * TILE, TILE), bf16),
        ],
        compiler_params=pltpu.CompilerParams(vmem_limit_bytes=60 * 2**20),
        cost_estimate=pl.CostEstimate(flops=5 * 10**10, bytes_accessed=16 * 2**20, transcendentals=3 * 10**7),
        name="grads",
    )(tiles, q, do, k, v, z, aux_r, aux_k)


MESH = pl.DeviceIdType.MESH
HEADS, INNER, OUTER, BLK, CTX_ROWS = 8, 4, 4, 128, 1024


def peers():
    head, inner, outer = (lax.axis_index(a) for a in ("head", "inner", "outer"))
    y_peer = lax.rem(inner + 2, INNER)
    core_peer = inner + 1 - 2 * lax.rem(inner, 2)
    x_next, x_prev = lax.rem(outer + 1, OUTER), lax.rem(outer + OUTER - 1, OUTER)
    return head, inner, outer, y_peer, core_peer, x_next, x_prev


def neighbours():
    head, inner, outer, y_peer, core_peer, x_next, x_prev = peers()
    across = (1 - head // 4) * 4
    return ([{"head": lax.rem(head + j, HEADS)} for j in range(1, HEADS)]
            + [{"head": across + z, "inner": y_peer} for z in range(4)]
            + [{"inner": y_peer}, {"inner": core_peer}, {"outer": x_next}, {"outer": x_prev}])


def greet(devices):
    barrier = pltpu.get_barrier_semaphore()
    for device in devices:
        pl.semaphore_signal(barrier, inc=1, device_id=device, device_id_type=MESH)
    pl.semaphore_wait(barrier, len(devices))


def rows_at(ref, block, chunk):
    return ref.at[pl.ds(pl.multiple_of(block * CTX_ROWS + chunk * BLK, BLK), BLK)]


def spread_kernel(q, do, k, v, out, pos, q_all, do_all, k_all, v_all, aux_r, aux_k,
                  aux, send1, recv1, send2, recv2, own_sem):
    head, inner, outer, y_peer, core_peer, x_next, x_prev = peers()
    greet(neighbours())

    def aux_at(ref, block, chunk):
        return ref.at[block, chunk]

    def fill_aux():
        for g in range(HEADS):
            aux[g, 2:8, :] = jnp.broadcast_to(pos[...].astype(f32), (6, BLK))
            for h in range(2):
                cols = slice((2 * g + h) * HD, (2 * g + h + 1) * HD)
                product = do[:, cols].astype(f32) * out[:, cols].astype(f32)
                aux[g, h:h + 1, :] = jnp.sum(product.T, axis=0, keepdims=True)

    def near(chunk):
        return chunk // 4 == head // 4

    def via(t, dest):
        if t in (0, 1, 4):
            return {"head": dest, "inner": jnp.where(near(dest), inner, y_peer)}
        return {"head": dest}

    def first(t, dest, source_head):
        if t == 4:
            return aux.at[dest], aux_at(aux_r, inner, source_head)
        if t == 5:
            return aux.at[dest], aux_at(aux_k, outer, source_head)
        src = (q, do, k, v)[t]
        dst = (q_all, do_all, k_all, v_all)[t]
        wide = 256 if t < 2 else 128
        return (src.at[:, pl.ds(pl.multiple_of(dest * wide, wide), wide)],
                rows_at(dst, inner if t < 2 else outer, source_head))

    def remote(src, dst, ssem, rsem, device):
        return pltpu.make_async_remote_copy(src_ref=src, dst_ref=dst, send_sem=ssem, recv_sem=rsem,
                                            device_id=device, device_id_type=MESH)

    ORDER = (0, 2, 4, 5, 3, 1)
    def send_part(part):
        for t in part:
            src, dst = first(t, head, head)
            pltpu.make_async_copy(src, dst, own_sem.at[t]).start()

        def send_first(j, _):
            dest = lax.rem(head + j, HEADS)
            for t in part:
                src, dst = first(t, dest, head)
                remote(src, dst, send1.at[t, dest], recv1.at[t, head], via(t, dest)).start()
            return 0

        lax.fori_loop(1, HEADS, send_first, 0)

    EARLY, LATE = (0, 2), (1, 3, 4, 5)
    send_part(EARLY)
    fill_aux()
    send_part(LATE)
    for t in ORDER:
        src, dst = first(t, head, head)
        pltpu.make_async_copy(src, dst, own_sem.at[t]).wait()

    def piece(t, block, chunk):
        if t == 4:
            return aux_at(aux_r, block, chunk)
        if t == 5:
            return aux_at(aux_k, block, chunk)
        return rows_at((q_all, do_all, k_all, v_all)[t], block, chunk)

    ROWS, KEYS = (0, 4, 1), (2, 5, 3)

    def hop(route, t, block, chunk, device):
        ref = piece(t, block, chunk)
        s = (ROWS if t in ROWS else KEYS).index(t)
        return remote(ref, ref, send2.at[route, s, chunk], recv2.at[route, s, chunk], device)

    Y, C, XN, XP = {"inner": y_peer}, {"inner": core_peer}, {"outer": x_next}, {"outer": x_prev}

    def forward(part, j):
        chunk = lax.rem(head + HEADS - j, HEADS)

        @pl.when(j > 0)
        def _():
            for t in part:
                src, dst = first(t, head, chunk)
                remote(src, dst, send1.at[t, chunk], recv1.at[t, chunk], {"head": chunk}).wait_recv()

        block = jnp.where(near(chunk), inner, y_peer)
        for t in part:
            if t in ROWS:
                hop(0, t, block, chunk, Y).start()
                hop(1, t, block, chunk, C).start()
            else:
                hop(3, t, outer, chunk, XN).start()
                hop(4, t, outer, chunk, XP).start()

    def relay(part, j):
        chunk = lax.rem(head + HEADS - j, HEADS)
        block = jnp.where(near(chunk), y_peer, inner)
        even = lax.rem(chunk, 2) == 0
        for t in part:
            if t in ROWS:
                hop(0, t, block, chunk, Y).wait_recv()
                hop(2, t, block, chunk, C).start()
        keys = [t for t in part if t in KEYS]
        for t in keys:
            hop(3, t, x_prev, chunk, XN).wait_recv()
            hop(4, t, x_next, chunk, XP).wait_recv()

        @pl.when(even)
        def _():
            for t in keys:
                hop(5, t, x_prev, chunk, XN).start()

        @pl.when(jnp.logical_not(even))
        def _():
            for t in keys:
                hop(5, t, x_next, chunk, XP).start()

    def steps(*calls):
        def step(j, _):
            for fn, part in calls:
                fn(part, j)
            return 0
        lax.fori_loop(0, HEADS, step, 0)

    steps((forward, EARLY))
    steps((forward, LATE), (relay, EARLY))
    steps((relay, LATE))
    y_core = lax.rem(core_peer + 2, INNER)
    x_far = lax.rem(outer + 2, OUTER)

    def finish(j, _):
        chunk = lax.rem(head + HEADS - j, HEADS)
        for t in ROWS:
            hop(1, t, core_peer, chunk, C).wait_recv()
            hop(2, t, y_core, chunk, C).wait_recv()
            hop(0, t, inner, chunk, Y).wait_send()
            hop(1, t, inner, chunk, C).wait_send()
            hop(2, t, y_peer, chunk, C).wait_send()
        for t in KEYS:
            hop(5, t, x_far, chunk, XN).wait_recv()
            hop(3, t, outer, chunk, XN).wait_send()
            hop(4, t, outer, chunk, XP).wait_send()
            hop(5, t, x_prev, chunk, XN).wait_send()

        @pl.when(j > 0)
        def _():
            for t in ORDER:
                src, dst = first(t, chunk, head)
                remote(src, dst, send1.at[t, chunk], recv1.at[t, chunk], {"head": chunk}).wait_send()
        return 0

    lax.fori_loop(0, HEADS, finish, 0)


def spread(q, do, k, v, out, pos):
    hbm = pl.BlockSpec(memory_space=pl.ANY)
    vm = pl.BlockSpec(memory_space=pltpu.VMEM)
    rows = INNER * CTX_ROWS
    return pl.pallas_call(
        spread_kernel,
        out_shape=(jax.ShapeDtypeStruct((rows, 256), bf16), jax.ShapeDtypeStruct((rows, 256), bf16),
                   jax.ShapeDtypeStruct((rows, 128), bf16), jax.ShapeDtypeStruct((rows, 128), bf16),
                   jax.ShapeDtypeStruct((INNER, HEADS, 8, 128), f32), jax.ShapeDtypeStruct((OUTER, HEADS, 8, 128), f32)),
        in_specs=[hbm, vm, hbm, hbm, vm, vm],
        out_specs=(hbm,) * 6,
        scratch_shapes=[pltpu.VMEM((HEADS, 8, 128), f32),
                        pltpu.SemaphoreType.DMA((6, HEADS)), pltpu.SemaphoreType.DMA((6, HEADS)),
                        pltpu.SemaphoreType.DMA((6, 3, HEADS)), pltpu.SemaphoreType.DMA((6, 3, HEADS)),
                        pltpu.SemaphoreType.DMA((6,))],
        compiler_params=pltpu.CompilerParams(collective_id=0, has_side_effects=True, vmem_limit_bytes=60 * 2**20),
        name="spread",
    )(q, do, k, v, out, pos)


def pool_kernel(z, out, recv, send_sem, recv_sem):
    head, inner, outer, y_peer, core_peer, x_next, x_prev = peers()
    others = [lax.rem(inner + j, INNER) for j in range(1, INNER)]
    greet([{"inner": o} for o in others])
    out[...] = jnp.sum(z[...], axis=2)
    copies = []
    for j, o in enumerate(others):
        copies.append(pltpu.make_async_remote_copy(
            src_ref=out, dst_ref=recv.at[j], send_sem=send_sem.at[j], recv_sem=recv_sem.at[j],
            device_id={"inner": o}, device_id_type=MESH))
        copies[-1].start()
    for c in copies:
        c.wait()
    total = jnp.zeros(out.shape, f32)
    for i in range(INNER):
        d = lax.rem(inner - i + INNER, INNER)
        part = jnp.where(d == 0, out[...], jnp.where(d == 1, recv[0], jnp.where(d == 2, recv[1], recv[2])))
        total = total + part
    out[...] = total


def pool(z):
    vm = pl.BlockSpec(memory_space=pltpu.VMEM)
    small = (z.shape[0], 2, z.shape[3])
    return pl.pallas_call(
        pool_kernel,
        out_shape=jax.ShapeDtypeStruct(small, f32),
        in_specs=[vm], out_specs=vm,
        scratch_shapes=[pltpu.VMEM((3,) + small, f32), pltpu.SemaphoreType.DMA((3,)), pltpu.SemaphoreType.DMA((3,))],
        compiler_params=pltpu.CompilerParams(collective_id=1, has_side_effects=True),
        name="pool",
    )(z)


def collect_kernel(dq, dk, dv, gq, gk, gv, q_near, kv_near, dq_pair, dq_sum, dq_far, kv_far, kv_relay, kv_sum,
                   low_q, low_k, low_v, send_sem, recv_sem, send_out, recv_out, own_sem):
    head, inner, outer, y_peer, core_peer, x_next, x_prev = peers()
    x_far = lax.rem(outer + 2, OUTER)

    def block_rows(block):
        return pl.ds(pl.multiple_of(block * CTX_ROWS, CTX_ROWS), CTX_ROWS)

    held = [pltpu.make_async_copy(dq.at[block_rows(y_peer)], q_near.at[1], own_sem.at[0]),
            pltpu.make_async_copy(dq.at[block_rows(inner)], q_near.at[0], own_sem.at[1])]
    for t in range(2):
        for x, block in enumerate((x_next, x_prev, outer)):
            held.append(pltpu.make_async_copy((dk, dv)[t].at[block_rows(block)], kv_near.at[t, x], own_sem.at[2 + 3 * t + x]))
    for copy in held:
        copy.start()
    greet(neighbours())
    y_core = lax.rem(core_peer + 2, INNER)
    Y, C, XN, XP = {"inner": y_peer}, {"inner": core_peer}, {"outer": x_next}, {"outer": x_prev}

    def remote(src, dst, ssem, rsem, device):
        return pltpu.make_async_remote_copy(src_ref=src, dst_ref=dst, send_sem=ssem, recv_sem=rsem,
                                            device_id=device, device_id_type=MESH)

    def local_rows(chunk):
        return pl.ds(pl.multiple_of(chunk * BLK, BLK), BLK)

    def near(chunk):
        return chunk // 4 == head // 4

    def pair_copy(which, chunk):
        block = jnp.where(near(chunk), *((core_peer, y_core) if which == 0 else (y_core, core_peer)))
        return remote(rows_at(dq, block, chunk), dq_pair.at[which, local_rows(chunk)],
                      send_sem.at[which, chunk], recv_sem.at[which, chunk], C)

    def far_copy(chunk):
        return remote(dq_sum.at[local_rows(chunk)], dq_far.at[local_rows(chunk)],
                      send_sem.at[2, chunk], recv_sem.at[2, chunk], Y)

    def kv_copy(t, x, chunk, device, summed=False):
        n = 3 + 3 * t + x
        src = kv_sum.at[t, local_rows(chunk)] if summed else rows_at((dk, dv)[t], (x_next, x_prev, x_far)[x], chunk)
        dst = kv_relay.at[t, local_rows(chunk)] if x == 2 else kv_far.at[t, x, local_rows(chunk)]
        return remote(src, dst, send_sem.at[n, chunk], recv_sem.at[n, chunk], device)

    def out_copy(t, chunk):
        low, out, wide = ((low_q, gq, 256), (low_k, gk, 128), (low_v, gv, 128))[t]
        device = {"head": chunk, "inner": jnp.where(near(chunk), inner, y_peer)} if t == 0 else {"head": chunk}
        return remote(low.at[local_rows(chunk)], out.at[:, pl.ds(pl.multiple_of(head * wide, wide), wide)],
                      send_out.at[t, chunk], recv_out.at[t, head], device)

    def chunk_at(j):
        return lax.rem(head + 1 + j, HEADS)

    def send_pair(j, _):
        chunk = chunk_at(j)
        even = lax.rem(chunk, 2) == 0

        @pl.when(even)
        def _():
            for t in range(2):
                kv_copy(t, 2, chunk, XN).start()

        @pl.when(jnp.logical_not(even))
        def _():
            for t in range(2):
                kv_copy(t, 2, chunk, XP).start()

        pair_copy(1, chunk).start()
        pair_copy(0, chunk).start()

        @pl.when(even)
        def _():
            for t in range(2):
                kv_copy(t, 1, chunk, XP).start()

        @pl.when(jnp.logical_not(even))
        def _():
            for t in range(2):
                kv_copy(t, 0, chunk, XN).start()
        return 0

    lax.fori_loop(0, HEADS, send_pair, 0)
    for copy in held:
        copy.wait()

    def sum_pair(j, _):
        chunk = chunk_at(j)
        rows = local_rows(chunk)
        pair_copy(1, chunk).wait_recv()
        mine = jnp.where(near(chunk), 0, 1)
        dq_sum[rows, :] = (q_near[1 - mine, rows, :].astype(f32) + dq_pair[1, rows, :].astype(f32)).astype(bf16)
        far_copy(chunk).start()
        odd = lax.rem(chunk, 2)
        for t in range(2):
            kv_copy(t, 2, chunk, XN).wait_recv()
            kv_sum[t, rows, :] = (kv_near[t, odd, rows, :].astype(f32) + kv_relay[t, rows, :].astype(f32)).astype(bf16)

        @pl.when(odd == 0)
        def _():
            for t in range(2):
                kv_copy(t, 0, chunk, XN, True).start()

        @pl.when(odd == 1)
        def _():
            for t in range(2):
                kv_copy(t, 1, chunk, XP, True).start()
        return 0

    lax.fori_loop(0, HEADS, sum_pair, 0)

    def sum_all(j, _):
        chunk = chunk_at(j)
        rows = local_rows(chunk)
        pair_copy(0, chunk).wait_recv()
        far_copy(chunk).wait_recv()
        mine = jnp.where(near(chunk), 0, 1)
        low_q[rows, :] = (q_near[mine, rows, :].astype(f32) + dq_pair[0, rows, :].astype(f32)
                          + dq_far[rows, :].astype(f32)).astype(bf16)
        pl.when(j < HEADS - 1)(lambda: out_copy(0, chunk).start())
        for t in range(2):
            total = kv_near[t, 2, rows, :].astype(f32)
            for x in range(2):
                kv_copy(t, x, chunk, XN).wait_recv()
                total = total + kv_far[t, x, rows, :].astype(f32)
            (low_k, low_v)[t][rows, :] = total.astype(bf16)

        @pl.when(j < HEADS - 1)
        def _():
            for t in (1, 2):
                out_copy(t, chunk).start()
        return 0

    lax.fori_loop(0, HEADS, sum_all, 0)
    own = []
    for t in range(3):
        low, out, wide = ((low_q, gq, 256), (low_k, gk, 128), (low_v, gv, 128))[t]
        own.append(pltpu.make_async_copy(low.at[local_rows(head)],
                                         out.at[:, pl.ds(pl.multiple_of(head * wide, wide), wide)], own_sem.at[t]))
        own[-1].start()

    def finish(j, _):
        chunk = chunk_at(j)
        for which in range(2):
            pair_copy(which, chunk).wait_send()
        far_copy(chunk).wait_send()
        for t in range(2):
            for x in range(3):
                kv_copy(t, x, chunk, XN).wait_send()

        @pl.when(j < HEADS - 1)
        def _():
            for t in range(3):
                low, out, wide = ((low_q, gq, 256), (low_k, gk, 128), (low_v, gv, 128))[t]
                out_copy(t, chunk).wait_send()
                remote(low.at[local_rows(head)], out.at[:, pl.ds(pl.multiple_of(chunk * wide, wide), wide)],
                       send_out.at[t, head], recv_out.at[t, chunk], {"head": chunk}).wait_recv()
        return 0

    lax.fori_loop(0, HEADS, finish, 0)
    for copy in own:
        copy.wait()


def collect(dq, dk, dv):
    hbm = pl.BlockSpec(memory_space=pl.ANY)
    wide, narrow = (CTX_ROWS, 256), (CTX_ROWS, 128)
    return pl.pallas_call(
        collect_kernel,
        out_shape=(jax.ShapeDtypeStruct((BLK, 2048), bf16), jax.ShapeDtypeStruct((BLK, 1024), bf16),
                   jax.ShapeDtypeStruct((BLK, 1024), bf16)),
        in_specs=[hbm] * 3,
        out_specs=(hbm,) * 3,
        scratch_shapes=[pltpu.VMEM((2,) + wide, bf16), pltpu.VMEM((2, 3) + narrow, bf16),
                        pltpu.VMEM((2,) + wide, bf16), pltpu.VMEM(wide, bf16), pltpu.VMEM(wide, bf16),
                        pltpu.VMEM((2, 2) + narrow, bf16), pltpu.VMEM((2,) + narrow, bf16), pltpu.VMEM((2,) + narrow, bf16),
                        pltpu.VMEM(wide, bf16), pltpu.VMEM(narrow, bf16), pltpu.VMEM(narrow, bf16),
                        pltpu.SemaphoreType.DMA((9, HEADS)), pltpu.SemaphoreType.DMA((9, HEADS)),
                        pltpu.SemaphoreType.DMA((3, HEADS)), pltpu.SemaphoreType.DMA((3, HEADS)),
                        pltpu.SemaphoreType.DMA((8,))],
        compiler_params=pltpu.CompilerParams(collective_id=2, has_side_effects=True, vmem_limit_bytes=60 * 2**20),
        name="collect",
    )(dq, dk, dv)


def local(queries, keys, values, output, grad_output, positions):
    q, do, k, v, aux_r, aux_k = spread(queries, grad_output, keys, values, output, positions.reshape(1, BLK))
    z, tiles = totals(q, k, aux_r, aux_k)
    dq, dk, dv = grads(tiles, q, do, k, v, pool(z), aux_r, aux_k)
    return collect(dq, dk, dv)


def solution(mesh):
    rows = P(("head", "inner", "outer"), None)
    return jax.shard_map(
        local, mesh=mesh,
        in_specs=(rows,) * 5 + (P(("head", "inner", "outer")),),
        out_specs=(rows,) * 3,
        check_vma=False,
    )
```

time: 227 us -> 185 us (0.81)
  Pallas kernels: 202 us -> 179 us
  other arithmetic: 9.27 us -> 0 us
  local copies, waits for them, and re-layouts: 13.2 us -> 5.22 us
    pallas_call x1, Pallas kernels: 75.4 us -> 61.5 us  [grads(): pl.pallas_call(functools.partial(grads_kernel, nr, nk), out_shape=(jax.Sh...]
    pallas_call x1, Pallas kernels: 53.8 us -> 47 us  [spread(): pl.pallas_call(spread_kernel, out_shape=(jax.ShapeDtypeStruct((rows, 256)...]
    convert_element_type x2 -> x0, local copies, waits for them, and re-layouts: 3.98 us -> none  [the longest x1 2 us: local(): kpos = aux_k[:, :, 2, :].reshape(-1).astype(jnp.int32)]
    reduce_min x3 -> x0, other arithmetic: 3.58 us -> none  [spans(): return jnp.stack([qb.min(1), qb.max(1), kb.min(1), kb.max(1)])]
    unnamed x13 -> x3, local copies, waits for them, and re-layouts: 6.25 us -> 5.22 us
where the time goes in v2:
time: 185 us
  Pallas kernels  179 us (97%)
  local copies, waits for them, and re-layouts  5.22 us (3%)
    pallas_call x1, Pallas kernels, grads(): pl.pallas_call(functools.partial(grads_kernel, nr, nk), out_shape=(jax.Sh...  61.5 us
    pallas_call x1, Pallas kernels, spread(): pl.pallas_call(spread_kernel, out_shape=(jax.ShapeDtypeStruct((rows, 256)...  47 us
    pallas_call x1, Pallas kernels, collect(): pl.pallas_call(collect_kernel, out_shape=(jax.ShapeDtypeStruct((BLK, 2048...  36.7 us
    pallas_call x1, Pallas kernels, totals(): pl.pallas_call(functools.partial(totals_kernel, nr, nk), out_shape=(jax.S...  28.1 us
    pallas_call x1, Pallas kernels, pool(): pl.pallas_call(pool_kernel, out_shape=jax.ShapeDtypeStruct(small, f32), i...  5.85 us
    unnamed x3, local copies, waits for them, and re-layouts  5.22 us

profile of v2, /device:TPU:64, one launch (start us, length us, event | category | flops | bytes accessed | tf_op | source)
XLA Modules:
  0.0 185.0 jit_solution(13501779356512856344)
XLA Ops:
  0.6 47.0 %spread.1 = (bf16[4096,256]{1,0:T(8,128)(2,1)}, bf16[4096,256]{1,0:T(8,128)(2,1)}, bf16[4096,128]{1,0:T(8,128)(2,1)}, bf16[4096,128]{1,0:T(8,128)(2,1)}, f32[4,8...) custom-call(bf16[128,2048]{1,0:T(8,128)(2,1)} %q.1, bf16[128,2048]{1,0:T(8,128)(2,1)} %do.1, bf16[128,1024]{1,0:T(8,128)(2,1)} %k.1, ...), custom_call_target="tpu_custom_call" | custom-call | tf_op jit(solution)/shard_map/spread/pallas_call | solution.py:398
  47.7 28.1 %totals.1 = (f32[8,2,8,512]{3,2,1,0:T(8,128)}, s32[72]{0:T(128)}) custom-call(bf16[4096,256]{1,0:T(8,128)(2,1)} %get-tuple-element.14.q_ref, bf16[4096,128]{1,0:T(8,128)(2,1)} %get-tuple-element.15.k_ref, f32[4,8,8,128]{3,2,1,0:T(8,128)} %get-tuple-element.16.aux_r, f32[4,8,8,128]{3,2,1,0:T(8,128)} %get-tuple-element.17.aux_k), custom_call_target="tpu_custom_call" | custom-call | flops 20000000000 | bytes 4194304 | tf_op jit(solution)/shard_map/totals/pallas_call | solution.py:97
  75.8 5.8 %pool.1.z_ref = f32[8,2,512]{2,1,0:T(2,128)} custom-call(f32[8,2,8,512]{3,2,1,0:T(8,128)} %get-tuple-element.21.z), custom_call_target="tpu_custom_call" | custom-call | tf_op jit(solution)/shard_map/pool/pallas_call | solution.py:438
  81.7 61.5 %grads.1 = (bf16[4096,256]{1,0:T(8,128)(2,1)}, bf16[4096,128]{1,0:T(8,128)(2,1)}, bf16[4096,128]{1,0:T(8,128)(2,1)}) custom-call(s32[72]{0:T(128)} %get-tuple-element.18.tiles, bf16[4096,256]{1,0:T(8,128)(2,1)} %get-tuple-element.14.q_ref, bf16[4096,256]{1,0:T(8,128)(2,1)} %get-tuple-element.19.do_ref, bf16[4096,128]{1,0:T(8,128)(2,1)} %get-tuple-element.15.k_ref, ...), custom_call_target="tpu_custom_call" | custom-call | flops 49999998976 | bytes 16777216 | tf_op jit(solution)/shard_map/grads/pallas_call | solution.py:188
  143.1 36.7 %collect.1 = (bf16[128,2048]{1,0:T(8,128)(2,1)}, bf16[128,1024]{1,0:T(8,128)(2,1)}, bf16[128,1024]{1,0:T(8,128)(2,1)}) custom-call(bf16[4096,256]{1,0:T(8,128)(2,1)} %get-tuple-element.22.dq, bf16[4096,128]{1,0:T(8,128)(2,1)} %get-tuple-element.23.dk, bf16[4096,128]{1,0:T(8,128)(2,1)} %get-tuple-element.24.dv), custom_call_target="tpu_custom_call" | custom-call | tf_op jit(solution)/shard_map/collect/pallas_call | solution.py:614
  179.8 1.9 %copy.12 = bf16[128,2048]{1,0:T(8,128)(2,1)} copy(bf16[128,2048]{1,0:T(8,128)(2,1)} %get-tuple-element.28) | data formatting | bytes 1048576
  181.7 1.7 copy.13
  183.3 1.7 copy.14

commit v3 on v2

--- a/solution.py
+++ b/solution.py
@@ -39,7 +39,7 @@
 WHOLE, PARTLY = 0, 4096
 
 
-def live_tiles(nr, nk, aux_r, aux_k, span, tiles):
+def live_tiles(nr, nk, aux_r, aux_k, span, tiles, rest):
     for b in range(nr):
         part = aux_r[b // 2, 4 * (b % 2):4 * (b % 2) + 4, 2, :]
         span[0, b] = jnp.min(part)
@@ -50,24 +50,31 @@
         span[3, b] = jnp.max(part)
     tiles[1] = nr * 64 + nk
 
-    def scan(i, n):
+    def scan(i, counts):
+        n, m = counts
         kb, rb = i // nr, lax.rem(i, nr)
         some = span[2, kb] <= span[1, rb]
         whole = span[3, kb] <= span[0, rb]
 
         @pl.when(some)
         def _():
-            tiles[n + 2] = jnp.where(whole, WHOLE, PARTLY) + rb * 64 + kb
-        return n + some.astype(jnp.int32)
-
-    n = lax.fori_loop(0, nr * nk, scan, 0)
+            code = jnp.where(whole, WHOLE, PARTLY) + rb * 64 + kb
+            tiles[n + 2] = code
+            rest[m] = code
+        step = some.astype(jnp.int32)
+        made = jnp.logical_and(lax.rem(rb, 2) == 1, lax.rem(kb, 2) == 0)
+        return n + step, m + jnp.where(made, 0, step)
+
+    n, m = lax.fori_loop(0, nr * nk, scan, (0, 0))
     tiles[0] = n
     tiles[n + 2] = nr * 64 + nk
-
-
-def totals_kernel(nr, nk, q_ref, k_ref, aux_r, aux_k, z_ref, tiles, span):
-    z_ref[...] = jnp.zeros_like(z_ref)
-    live_tiles(nr, nk, aux_r, aux_k, span, tiles)
+    return m
+
+
+def totals_kernel(nr, nk, q_ref, k_ref, aux_r, aux_k, part_ref, z_ref, tiles, span, rest):
+    for b in range(nr):
+        z_ref[b] = part_ref[b // 2] if b % 2 else jnp.zeros((2, 8, TILE), f32)
+    count = live_tiles(nr, nk, aux_r, aux_k, span, tiles, rest)
 
     def tile(rb, kb, masked):
         rows = pl.ds(pl.multiple_of(rb * TILE, TILE), TILE)
@@ -82,28 +89,28 @@
             z_ref[rb, h] += jnp.sum(e.reshape(TILE // 8, 8, TILE), axis=0)
 
     def step(i, _):
-        code = tiles[i + 2]
+        code = rest[i]
         rb, kb = (code // 64) % 64, code % 64
         pl.when(code < PARTLY)(lambda: tile(rb, kb, False))
         pl.when(code >= PARTLY)(lambda: tile(rb, kb, True))
         return 0
 
-    lax.fori_loop(0, tiles[0], step, 0)
-
-
-def totals(q, k, aux_r, aux_k):
+    lax.fori_loop(0, count, step, 0)
+
+
+def totals(q, k, aux_r, aux_k, part):
     nr, nk = q.shape[0] // TILE, k.shape[0] // TILE
     vm = pl.BlockSpec(memory_space=pltpu.VMEM)
     return pl.pallas_call(
         functools.partial(totals_kernel, nr, nk),
         out_shape=(jax.ShapeDtypeStruct((nr, 2, 8, TILE), f32), jax.ShapeDtypeStruct((nr * nk + 8,), jnp.int32)),
-        in_specs=[vm, vm, vm, vm],
+        in_specs=[vm] * 5,
         out_specs=(vm, pl.BlockSpec(memory_space=pltpu.SMEM)),
-        scratch_shapes=[pltpu.SMEM((4, 8), f32)],
+        scratch_shapes=[pltpu.SMEM((4, 8), f32), pltpu.SMEM((nr * nk + 8,), jnp.int32)],
         compiler_params=pltpu.CompilerParams(vmem_limit_bytes=60 * 2**20),
         cost_estimate=pl.CostEstimate(flops=2 * 10**10, bytes_accessed=4 * 2**20, transcendentals=3 * 10**7),
         name="totals",
-    )(q, k, aux_r, aux_k)
+    )(q, k, aux_r, aux_k, part)
 
 
 def grads_kernel(nr, nk, tiles, q_ref, do_ref, k_ref, v_ref, z_ref, aux_r, aux_k,
@@ -235,7 +242,7 @@
     return ref.at[pl.ds(pl.multiple_of(block * CTX_ROWS + chunk * BLK, BLK), BLK)]
 
 
-def spread_kernel(q, do, k, v, out, pos, q_all, do_all, k_all, v_all, aux_r, aux_k,
+def spread_kernel(q, do, k, v, out, pos, q_all, do_all, k_all, v_all, aux_r, aux_k, z_ref,
                   aux, send1, recv1, send2, recv2, own_sem):
     head, inner, outer, y_peer, core_peer, x_next, x_prev = peers()
     greet(neighbours())
@@ -289,106 +296,132 @@
 
         lax.fori_loop(1, HEADS, send_first, 0)
 
-    EARLY, LATE = (0, 2), (1, 3, 4, 5)
-    send_part(EARLY)
+    EARLY, LATE = (0, 2, 4, 5), (1, 3)
+    send_part((0, 2))
     fill_aux()
+    send_part((4, 5))
     send_part(LATE)
-    for t in ORDER:
-        src, dst = first(t, head, head)
-        pltpu.make_async_copy(src, dst, own_sem.at[t]).wait()
-
-    def piece(t, block, chunk):
-        if t == 4:
-            return aux_at(aux_r, block, chunk)
-        if t == 5:
-            return aux_at(aux_k, block, chunk)
-        return rows_at((q_all, do_all, k_all, v_all)[t], block, chunk)
+
+    def wait_own(part):
+        for t in part:
+            src, dst = first(t, head, head)
+            pltpu.make_async_copy(src, dst, own_sem.at[t]).wait()
+
+    wait_own(EARLY)
+
+    y_core = lax.rem(core_peer + 2, INNER)
+    x_far = lax.rem(outer + 2, OUTER)
+
+    def base(g):
+        return 4 * (head // 4) if g == 0 else 4 * (1 - head // 4)
+
+    def piece(t, block, g):
+        if t >= 4:
+            return (aux_r, aux_k)[t - 4].at[block, pl.ds(base(g), 4)]
+        return (q_all, do_all, k_all, v_all)[t].at[pl.ds(pl.multiple_of(block * CTX_ROWS + base(g) * BLK, 4 * BLK), 4 * BLK)]
 
     ROWS, KEYS = (0, 4, 1), (2, 5, 3)
 
-    def hop(route, t, block, chunk, device):
-        ref = piece(t, block, chunk)
+    def hop(route, t, block, g, device):
+        ref = piece(t, block, g)
         s = (ROWS if t in ROWS else KEYS).index(t)
-        return remote(ref, ref, send2.at[route, s, chunk], recv2.at[route, s, chunk], device)
+        return remote(ref, ref, send2.at[route, s, g], recv2.at[route, s, g], device)
 
     Y, C, XN, XP = {"inner": y_peer}, {"inner": core_peer}, {"outer": x_next}, {"outer": x_prev}
 
-    def forward(part, j):
-        chunk = lax.rem(head + HEADS - j, HEADS)
-
-        @pl.when(j > 0)
-        def _():
+    def forward(part, g):
+        def wait_first(chunk):
             for t in part:
                 src, dst = first(t, head, chunk)
                 remote(src, dst, send1.at[t, chunk], recv1.at[t, chunk], {"head": chunk}).wait_recv()
 
-        block = jnp.where(near(chunk), inner, y_peer)
+        for n in range(4):
+            chunk = base(g) + lax.rem(head + 4 - n, 4)
+            if g == 1 or n > 0:
+                wait_first(chunk)
         for t in part:
             if t in ROWS:
-                hop(0, t, block, chunk, Y).start()
-                hop(1, t, block, chunk, C).start()
+                block = inner if g == 0 else y_peer
+                hop(0, t, block, g, Y).start()
+                hop(1, t, block, g, C).start()
             else:
-                hop(3, t, outer, chunk, XN).start()
-                hop(4, t, outer, chunk, XP).start()
-
-    def relay(part, j):
-        chunk = lax.rem(head + HEADS - j, HEADS)
-        block = jnp.where(near(chunk), y_peer, inner)
-        even = lax.rem(chunk, 2) == 0
+                hop(3, t, outer, g, XN).start()
+                hop(4, t, outer, g, XP).start()
+
+    def relay(part, g):
         for t in part:
             if t in ROWS:
-                hop(0, t, block, chunk, Y).wait_recv()
-                hop(2, t, block, chunk, C).start()
-        keys = [t for t in part if t in KEYS]
-        for t in keys:
-            hop(3, t, x_prev, chunk, XN).wait_recv()
-            hop(4, t, x_next, chunk, XP).wait_recv()
-
-        @pl.when(even)
-        def _():
-            for t in keys:
-                hop(5, t, x_prev, chunk, XN).start()
-
-        @pl.when(jnp.logical_not(even))
-        def _():
-            for t in keys:
-                hop(5, t, x_next, chunk, XP).start()
-
-    def steps(*calls):
-        def step(j, _):
-            for fn, part in calls:
-                fn(part, j)
+                block = y_peer if g == 0 else inner
+                hop(0, t, block, g, Y).wait_recv()
+                hop(2, t, block, g, C).start()
+        for t in part:
+            if t in KEYS:
+                hop(3, t, x_prev, g, XN).wait_recv()
+                hop(4, t, x_next, g, XP).wait_recv()
+                if g == 0:
+                    hop(5, t, x_prev, g, XN).start()
+                else:
+                    hop(5, t, x_next, g, XP).start()
+
+    def arrive(part):
+        for g in range(2):
+            for t in part:
+                if t in ROWS:
+                    hop(1, t, core_peer, g, C).wait_recv()
+                    hop(2, t, y_core, g, C).wait_recv()
+                else:
+                    hop(5, t, x_far, g, XN).wait_recv()
+
+    def tile(n):
+        r, c = n // 4, lax.rem(n, 4)
+        live = widen(column(place_of(aux_k, 2 * c))) <= place_of(aux_r, 2 * r + 1)
+        kk = k_all[pl.ds(pl.multiple_of(c * CTX_ROWS, CTX_ROWS), TILE), :]
+        rows = pl.ds(pl.multiple_of(r * CTX_ROWS + TILE, TILE), TILE)
+        for h in range(2):
+            e = jnp.exp2(jnp.tanh(nt(kk, q_all[rows, h * HD:(h + 1) * HD]) * SCALE) * CAP2)
+            z_ref[r, h] += jnp.sum(jnp.where(live, e, 0.0).reshape(TILE // 8, 8, TILE), axis=0)
+
+    def some_tiles(start, stop):
+        def step(n, _):
+            tile(n)
             return 0
-        lax.fori_loop(0, HEADS, step, 0)
-
-    steps((forward, EARLY))
-    steps((forward, LATE), (relay, EARLY))
-    steps((relay, LATE))
-    y_core = lax.rem(core_peer + 2, INNER)
-    x_far = lax.rem(outer + 2, OUTER)
+        lax.fori_loop(start, stop, step, 0)
+
+    forward(EARLY, 0)
+    forward(EARLY, 1)
+    z_ref[...] = jnp.zeros_like(z_ref)
+    wait_own(LATE)
+    relay(EARLY, 0)
+    forward(LATE, 0)
+    relay(EARLY, 1)
+    arrive(EARLY)
+    some_tiles(0, 4)
+    forward(LATE, 1)
+    some_tiles(4, 8)
+    relay(LATE, 0)
+    some_tiles(8, 14)
+    relay(LATE, 1)
+    some_tiles(14, 16)
+    arrive(LATE)
+
+    for g in range(2):
+        for t in ROWS:
+            hop(0, t, inner, g, Y).wait_send()
+            hop(1, t, inner, g, C).wait_send()
+            hop(2, t, y_peer, g, C).wait_send()
+        for t in KEYS:
+            hop(3, t, outer, g, XN).wait_send()
+            hop(4, t, outer, g, XP).wait_send()
+            hop(5, t, x_prev, g, XN).wait_send()
 
     def finish(j, _):
         chunk = lax.rem(head + HEADS - j, HEADS)
-        for t in ROWS:
-            hop(1, t, core_peer, chunk, C).wait_recv()
-            hop(2, t, y_core, chunk, C).wait_recv()
-            hop(0, t, inner, chunk, Y).wait_send()
-            hop(1, t, inner, chunk, C).wait_send()
-            hop(2, t, y_peer, chunk, C).wait_send()
-        for t in KEYS:
-            hop(5, t, x_far, chunk, XN).wait_recv()
-            hop(3, t, outer, chunk, XN).wait_send()
-            hop(4, t, outer, chunk, XP).wait_send()
-            hop(5, t, x_prev, chunk, XN).wait_send()
-
-        @pl.when(j > 0)
-        def _():
-            for t in ORDER:
-                src, dst = first(t, chunk, head)
-                remote(src, dst, send1.at[t, chunk], recv1.at[t, chunk], {"head": chunk}).wait_send()
-        return 0
-
-    lax.fori_loop(0, HEADS, finish, 0)
+        for t in ORDER:
+            src, dst = first(t, chunk, head)
+            remote(src, dst, send1.at[t, chunk], recv1.at[t, chunk], {"head": chunk}).wait_send()
+        return 0
+
+    lax.fori_loop(1, HEADS, finish, 0)
 
 
 def spread(q, do, k, v, out, pos):
@@ -399,12 +432,13 @@
         spread_kernel,
         out_shape=(jax.ShapeDtypeStruct((rows, 256), bf16), jax.ShapeDtypeStruct((rows, 256), bf16),
                    jax.ShapeDtypeStruct((rows, 128), bf16), jax.ShapeDtypeStruct((rows, 128), bf16),
-                   jax.ShapeDtypeStruct((INNER, HEADS, 8, 128), f32), jax.ShapeDtypeStruct((OUTER, HEADS, 8, 128), f32)),
-        in_specs=[hbm, vm, hbm, hbm, vm, vm],
-        out_specs=(hbm,) * 6,
+                   jax.ShapeDtypeStruct((INNER, HEADS, 8, 128), f32), jax.ShapeDtypeStruct((OUTER, HEADS, 8, 128), f32),
+                   jax.ShapeDtypeStruct((INNER, 2, 8, TILE), f32)),
+        in_specs=[vm] * 6,
+        out_specs=(vm, hbm, vm, hbm, vm, vm, vm),
         scratch_shapes=[pltpu.VMEM((HEADS, 8, 128), f32),
                         pltpu.SemaphoreType.DMA((6, HEADS)), pltpu.SemaphoreType.DMA((6, HEADS)),
-                        pltpu.SemaphoreType.DMA((6, 3, HEADS)), pltpu.SemaphoreType.DMA((6, 3, HEADS)),
+                        pltpu.SemaphoreType.DMA((6, 3, 2)), pltpu.SemaphoreType.DMA((6, 3, 2)),
                         pltpu.SemaphoreType.DMA((6,))],
         compiler_params=pltpu.CompilerParams(collective_id=0, has_side_effects=True, vmem_limit_bytes=60 * 2**20),
         name="spread",
@@ -629,11 +663,28 @@
     )(dq, dk, dv)
 
 
+def hand_over_kernel(a, b, c, x, y, z):
+    x[...] = a[...]
+    y[...] = b[...]
+    z[...] = c[...]
+
+
+def hand_over(*arrays):
+    vm = pl.BlockSpec(memory_space=pltpu.VMEM)
+    return pl.pallas_call(
+        hand_over_kernel,
+        out_shape=tuple(jax.ShapeDtypeStruct(a.shape, a.dtype) for a in arrays),
+        in_specs=[vm] * 3, out_specs=(vm,) * 3,
+        compiler_params=pltpu.CompilerParams(vmem_limit_bytes=60 * 2**20),
+        name="hand_over",
+    )(*arrays)
+
+
 def local(queries, keys, values, output, grad_output, positions):
-    q, do, k, v, aux_r, aux_k = spread(queries, grad_output, keys, values, output, positions.reshape(1, BLK))
-    z, tiles = totals(q, k, aux_r, aux_k)
+    q, do, k, v, aux_r, aux_k, part = spread(queries, grad_output, keys, values, output, positions.reshape(1, BLK))
+    z, tiles = totals(q, k, aux_r, aux_k, part)
     dq, dk, dv = grads(tiles, q, do, k, v, pool(z), aux_r, aux_k)
-    return collect(dq, dk, dv)
+    return hand_over(*collect(dq, dk, dv))
 
 
 def solution(mesh):

time: 185 us -> 181 us (0.978)
  local copies, waits for them, and re-layouts: 5.22 us -> 0 us
    pallas_call x1, Pallas kernels: 28.1 us -> 16.7 us  [totals(): pl.pallas_call(functools.partial(totals_kernel, nr, nk), out_shape=(jax.S...]
    pallas_call x1, Pallas kernels: 47 us -> 57.1 us  [spread(): pl.pallas_call(spread_kernel, out_shape=(jax.ShapeDtypeStruct((rows, 256)...]
    unnamed x3 -> x0, local copies, waits for them, and re-layouts: 5.22 us -> none
    pallas_call x0 -> x1, Pallas kernels: none -> 2.17 us  [hand_over(): pl.pallas_call(hand_over_kernel, out_shape=tuple((jax.ShapeDtypeStruct(a....]
where the time goes in v3:
time: 181 us; the launch traced here: 180 us
  Pallas kernels  179 us (99%)
    pallas_call x1, Pallas kernels, grads(): pl.pallas_call(functools.partial(grads_kernel, nr, nk), out_shape=(jax.Sh...  61.5 us
    pallas_call x1, Pallas kernels, spread(): pl.pallas_call(spread_kernel, out_shape=(jax.ShapeDtypeStruct((rows, 256)...  57.1 us
    pallas_call x1, Pallas kernels, collect(): pl.pallas_call(collect_kernel, out_shape=(jax.ShapeDtypeStruct((BLK, 2048...  35.8 us
    pallas_call x1, Pallas kernels, totals(): pl.pallas_call(functools.partial(totals_kernel, nr, nk), out_shape=(jax.S...  16.7 us
    pallas_call x1, Pallas kernels, pool(): pl.pallas_call(pool_kernel, out_shape=jax.ShapeDtypeStruct(small, f32), i...  5.85 us

profile of v3, /device:TPU:64, one launch (start us, length us, event | category | flops | bytes accessed | tf_op | source)
XLA Modules:
  0.0 179.8 jit_solution(4449936884526759691)
XLA Ops:
  0.6 57.1 %spread.1 = (bf16[4096,256]{1,0:T(8,128)(2,1)}, bf16[4096,256]{1,0:T(8,128)(2,1)}, bf16[4096,128]{1,0:T(8,128)(2,1)}, bf16[4096,128]{1,0:T(8,128)(2,1)}, f32[4,8...) custom-call(bf16[128,2048]{1,0:T(8,128)(2,1)} %q.1, bf16[128,2048]{1,0:T(8,128)(2,1)} %do.1, ...), custom_call_target="tpu_custom_call" | custom-call | tf_op jit(solution)/shard_map/spread/pallas_call | solution.py:431
  57.7 16.7 %totals.1 = (f32[8,2,8,512]{3,2,1,0:T(8,128)}, s32[72]{0:T(128)}) custom-call(bf16[4096,256]{1,0:T(8,128)(2,1)} %get-tuple-element.18.q_ref, bf16[4096,128]{1,0:T(8,128)(2,1)} %get-tuple-element.19.k_ref, f32[4,8,8,128]{3,2,1,0:T(8,128)} %get-tuple-element.20.aux_r, f32[4,8,8,128]{3,2,1,0:T(8,128)} %get-tuple-element.21.aux_k, ...), custom_call_target="tpu_custom_call" | custom-call | flops 20000000000 | bytes 4194304 | tf_op jit(solution)/shard_map/totals/pallas_call | solution.py:104
  74.5 5.8 %pool.1.z_ref = f32[8,2,512]{2,1,0:T(2,128)} custom-call(f32[8,2,8,512]{3,2,1,0:T(8,128)} %get-tuple-element.26.z), custom_call_target="tpu_custom_call" | custom-call | tf_op jit(solution)/shard_map/pool/pallas_call | solution.py:472
  80.4 61.5 %grads.1 = (bf16[4096,256]{1,0:T(8,128)(2,1)}, bf16[4096,128]{1,0:T(8,128)(2,1)}, bf16[4096,128]{1,0:T(8,128)(2,1)}) custom-call(s32[72]{0:T(128)} %get-tuple-element.23.tiles, bf16[4096,256]{1,0:T(8,128)(2,1)} %get-tuple-element.18.q_ref, bf16[4096,256]{1,0:T(8,128)(2,1)} %get-tuple-element.24.do_ref, bf16[4096,128]{1,0:T(8,128)(2,1)} %get-tuple-element.19.k_ref, ...), custom_call_target="tpu_custom_call" | custom-call | flops 49999998976 | bytes 16777216 | tf_op jit(solution)/shard_map/grads/pallas_call | solution.py:195
  141.8 35.8 %collect.1 = (bf16[128,2048]{1,0:T(8,128)(2,1)}, bf16[128,1024]{1,0:T(8,128)(2,1)}, bf16[128,1024]{1,0:T(8,128)(2,1)}) custom-call(bf16[4096,256]{1,0:T(8,128)(2,1)} %get-tuple-element.27.dq, bf16[4096,128]{1,0:T(8,128)(2,1)} %get-tuple-element.28.dk, bf16[4096,128]{1,0:T(8,128)(2,1)} %get-tuple-element.29.dv), custom_call_target="tpu_custom_call" | custom-call | tf_op jit(solution)/shard_map/collect/pallas_call | solution.py:648
  177.6 2.2 %hand_over.1 = (bf16[128,2048]{1,0:T(8,128)(2,1)}, bf16[128,1024]{1,0:T(8,128)(2,1)}, bf16[128,1024]{1,0:T(8,128)(2,1)}) custom-call(bf16[128,2048]{1,0:T(8,128)(2,1)} %get-tuple-element.30.a, bf16[128,1024]{1,0:T(8,128)(2,1)} %get-tuple-element.31.b, bf16[128,1024]{1,0:T(8,128)(2,1)} %get-tuple-element.32.c), custom_call_target="tpu_custom_call" | custom-call | tf_op jit(solution)/shard_map/hand_over/pallas_call | solution.py:674

commit v4 on v3

--- a/solution.py
+++ b/solution.py
@@ -114,7 +114,7 @@
 
 
 def grads_kernel(nr, nk, tiles, q_ref, do_ref, k_ref, v_ref, z_ref, aux_r, aux_k,
-                 dq_ref, dk_ref, dv_ref, qs, dos, qt, dot, dq, dkt, dvt, lcol, dcol, wbuf, gbuf):
+                 dq_ref, dk_ref, dv_ref, qt, dot, dq, dkt, dvt, lcol, dcol, wbuf, gbuf):
     dq[...] = jnp.zeros_like(dq)
     dkt[...] = jnp.zeros_like(dkt)
     dvt[...] = jnp.zeros_like(dvt)
@@ -124,8 +124,6 @@
         for h in range(2):
             cols = slice(h * HD, (h + 1) * HD)
             hr = slice(h * TILE, (h + 1) * TILE)
-            qs[rb, hr, :] = q_ref[rows, cols]
-            dos[rb, hr, :] = do_ref[rows, cols]
             qt[rb, :, hr] = q_ref[rows, cols].T
             dot[rb, :, hr] = do_ref[rows, cols].T
             lcol[rb, hr, :] = column(jnp.log2(z_ref[rb, h:h + 1, :]))
@@ -153,8 +151,10 @@
             dv_sum = dv_sum + nn(dot[rc, :, hr], w)
             dk_sum = dk_sum + nn(qt[rc, :, hr], g)
             dq[rc, hr, :] += nn(g, kcc)
-            t = jnp.tanh(nt(qs[ra, hr, :], kk) * SCALE)
-            p = nt(dos[ra, hr, :], vv)
+            rows = pl.ds(pl.multiple_of(ra * TILE + c * STRIP % TILE, STRIP), STRIP)
+            cols = slice(c * STRIP // TILE * HD, (c * STRIP // TILE + 1) * HD)
+            t = jnp.tanh(nt(q_ref[rows, cols], kk) * SCALE)
+            p = nt(do_ref[rows, cols], vv)
             w = jnp.exp2(t * CAP2 - widen(lcol[ra, hr, :]))
             if masked:
                 lo = c * STRIP % TILE
@@ -198,7 +198,6 @@
         in_specs=[pl.BlockSpec(memory_space=pltpu.SMEM)] + [vm] * 7,
         out_specs=(vm,) * 3,
         scratch_shapes=[
-            pltpu.VMEM((nr, 2 * TILE, HD), bf16), pltpu.VMEM((nr, 2 * TILE, HD), bf16),
             pltpu.VMEM((nr + 1, HD, 2 * TILE), bf16), pltpu.VMEM((nr + 1, HD, 2 * TILE), bf16),
             pltpu.VMEM((nr + 1, 2 * TILE, HD), f32),
             pltpu.VMEM((nk + 1, HD, TILE), f32), pltpu.VMEM((nk + 1, HD, TILE), f32),
@@ -394,14 +393,13 @@
     relay(EARLY, 0)
     forward(LATE, 0)
     relay(EARLY, 1)
+    forward(LATE, 1)
     arrive(EARLY)
     some_tiles(0, 4)
-    forward(LATE, 1)
-    some_tiles(4, 8)
     relay(LATE, 0)
-    some_tiles(8, 14)
+    some_tiles(4, 10)
     relay(LATE, 1)
-    some_tiles(14, 16)
+    some_tiles(10, 16)
     arrive(LATE)
 
     for g in range(2):
@@ -532,65 +530,48 @@
     def chunk_at(j):
         return lax.rem(head + 1 + j, HEADS)
 
-    def send_pair(j, _):
-        chunk = chunk_at(j)
-        even = lax.rem(chunk, 2) == 0
-
-        @pl.when(even)
-        def _():
-            for t in range(2):
-                kv_copy(t, 2, chunk, XN).start()
-
-        @pl.when(jnp.logical_not(even))
-        def _():
-            for t in range(2):
-                kv_copy(t, 2, chunk, XP).start()
-
+    def each_chunk(fn):
+        def step(j, _):
+            fn(j, chunk_at(j))
+            return 0
+        lax.fori_loop(0, HEADS, step, 0)
+
+    def by_parity(chunk, even, odd):
+        pl.when(lax.rem(chunk, 2) == 0)(lambda: [even(t) for t in range(2)] and None)
+        pl.when(lax.rem(chunk, 2) == 1)(lambda: [odd(t) for t in range(2)] and None)
+
+    def send_through(j, chunk):
         pair_copy(1, chunk).start()
+        by_parity(chunk, lambda t: kv_copy(t, 2, chunk, XN).start(), lambda t: kv_copy(t, 2, chunk, XP).start())
+
+    def send_direct(j, chunk):
         pair_copy(0, chunk).start()
-
-        @pl.when(even)
-        def _():
-            for t in range(2):
-                kv_copy(t, 1, chunk, XP).start()
-
-        @pl.when(jnp.logical_not(even))
-        def _():
-            for t in range(2):
-                kv_copy(t, 0, chunk, XN).start()
-        return 0
-
-    lax.fori_loop(0, HEADS, send_pair, 0)
+        by_parity(chunk, lambda t: kv_copy(t, 1, chunk, XP).start(), lambda t: kv_copy(t, 0, chunk, XN).start())
+
+    each_chunk(send_through)
+    each_chunk(send_direct)
     for copy in held:
         copy.wait()
 
-    def sum_pair(j, _):
-        chunk = chunk_at(j)
+    def sum_pair(j, chunk):
         rows = local_rows(chunk)
         pair_copy(1, chunk).wait_recv()
         mine = jnp.where(near(chunk), 0, 1)
         dq_sum[rows, :] = (q_near[1 - mine, rows, :].astype(f32) + dq_pair[1, rows, :].astype(f32)).astype(bf16)
         far_copy(chunk).start()
+
+    def sum_relay(j, chunk):
+        rows = local_rows(chunk)
         odd = lax.rem(chunk, 2)
         for t in range(2):
             kv_copy(t, 2, chunk, XN).wait_recv()
             kv_sum[t, rows, :] = (kv_near[t, odd, rows, :].astype(f32) + kv_relay[t, rows, :].astype(f32)).astype(bf16)
-
-        @pl.when(odd == 0)
-        def _():
-            for t in range(2):
-                kv_copy(t, 0, chunk, XN, True).start()
-
-        @pl.when(odd == 1)
-        def _():
-            for t in range(2):
-                kv_copy(t, 1, chunk, XP, True).start()
-        return 0
-
-    lax.fori_loop(0, HEADS, sum_pair, 0)
-
-    def sum_all(j, _):
-        chunk = chunk_at(j)
+        by_parity(chunk, lambda t: kv_copy(t, 0, chunk, XN, True).start(), lambda t: kv_copy(t, 1, chunk, XP, True).start())
+
+    each_chunk(sum_pair)
+    each_chunk(sum_relay)
+
+    def finish_rows(j, chunk):
         rows = local_rows(chunk)
         pair_copy(0, chunk).wait_recv()
         far_copy(chunk).wait_recv()
@@ -598,6 +579,9 @@
         low_q[rows, :] = (q_near[mine, rows, :].astype(f32) + dq_pair[0, rows, :].astype(f32)
                           + dq_far[rows, :].astype(f32)).astype(bf16)
         pl.when(j < HEADS - 1)(lambda: out_copy(0, chunk).start())
+
+    def finish_keys(j, chunk):
+        rows = local_rows(chunk)
         for t in range(2):
             total = kv_near[t, 2, rows, :].astype(f32)
             for x in range(2):
@@ -609,9 +593,12 @@
         def _():
             for t in (1, 2):
                 out_copy(t, chunk).start()
-        return 0
-
-    lax.fori_loop(0, HEADS, sum_all, 0)
+
+    def finish_both(j, chunk):
+        finish_rows(j, chunk)
+        finish_keys(j, chunk)
+
+    each_chunk(finish_both)
     own = []
     for t in range(3):
         low, out, wide = ((low_q, gq, 256), (low_k, gk, 128), (low_v, gv, 128))[t]

time: 181 us -> 177 us (0.978)
  Pallas kernels: 179 us -> 176 us
    pallas_call x1, Pallas kernels: 57.1 us -> 54.1 us  [spread(): pl.pallas_call(spread_kernel, out_shape=(jax.ShapeDtypeStruct((rows, 256)...]
where the time goes in v4:
time: 177 us
  Pallas kernels  176 us (99%)
    pallas_call x1, Pallas kernels, grads(): pl.pallas_call(functools.partial(grads_kernel, nr, nk), out_shape=(jax.Sh...  60.9 us
    pallas_call x1, Pallas kernels, spread(): pl.pallas_call(spread_kernel, out_shape=(jax.ShapeDtypeStruct((rows, 256)...  54.1 us
    pallas_call x1, Pallas kernels, collect(): pl.pallas_call(collect_kernel, out_shape=(jax.ShapeDtypeStruct((BLK, 2048...  36.3 us
    pallas_call x1, Pallas kernels, totals(): pl.pallas_call(functools.partial(totals_kernel, nr, nk), out_shape=(jax.S...  16.7 us
    pallas_call x1, Pallas kernels, pool(): pl.pallas_call(pool_kernel, out_shape=jax.ShapeDtypeStruct(small, f32), i...  5.85 us

profile of v4, /device:TPU:64, one launch (start us, length us, event | category | flops | bytes accessed | tf_op | source)
XLA Modules:
  0.0 176.7 jit_solution(13113053209040561246)
XLA Ops:
  0.6 54.1 %spread.1 = (bf16[4096,256]{1,0:T(8,128)(2,1)}, bf16[4096,256]{1,0:T(8,128)(2,1)}, bf16[4096,128]{1,0:T(8,128)(2,1)}, bf16[4096,128]{1,0:T(8,128)(2,1)}, f32[4,8...) custom-call(bf16[128,2048]{1,0:T(8,128)(2,1)} %q.1, bf16[128,2048]{1,0:T(8,128)(2,1)} %do.1, ...), custom_call_target="tpu_custom_call" | custom-call | tf_op jit(solution)/shard_map/spread/pallas_call | solution.py:429
  54.7 16.7 %totals.1 = (f32[8,2,8,512]{3,2,1,0:T(8,128)}, s32[72]{0:T(128)}) custom-call(bf16[4096,256]{1,0:T(8,128)(2,1)} %get-tuple-element.18.q_ref, bf16[4096,128]{1,0:T(8,128)(2,1)} %get-tuple-element.19.k_ref, f32[4,8,8,128]{3,2,1,0:T(8,128)} %get-tuple-element.20.aux_r, f32[4,8,8,128]{3,2,1,0:T(8,128)} %get-tuple-element.21.aux_k, ...), custom_call_target="tpu_custom_call" | custom-call | flops 20000000000 | bytes 4194304 | tf_op jit(solution)/shard_map/totals/pallas_call | solution.py:104
  71.5 5.8 %pool.1.z_ref = f32[8,2,512]{2,1,0:T(2,128)} custom-call(f32[8,2,8,512]{3,2,1,0:T(8,128)} %get-tuple-element.26.z), custom_call_target="tpu_custom_call" | custom-call | tf_op jit(solution)/shard_map/pool/pallas_call | solution.py:470
  77.3 60.9 %grads.1 = (bf16[4096,256]{1,0:T(8,128)(2,1)}, bf16[4096,128]{1,0:T(8,128)(2,1)}, bf16[4096,128]{1,0:T(8,128)(2,1)}) custom-call(s32[72]{0:T(128)} %get-tuple-element.23.tiles, bf16[4096,256]{1,0:T(8,128)(2,1)} %get-tuple-element.18.q_ref, bf16[4096,256]{1,0:T(8,128)(2,1)} %get-tuple-element.24.do_ref, bf16[4096,128]{1,0:T(8,128)(2,1)} %get-tuple-element.19.k_ref, ...), custom_call_target="tpu_custom_call" | custom-call | flops 49999998976 | bytes 16777216 | tf_op jit(solution)/shard_map/grads/pallas_call | solution.py:195
  138.2 36.3 %collect.1 = (bf16[128,2048]{1,0:T(8,128)(2,1)}, bf16[128,1024]{1,0:T(8,128)(2,1)}, bf16[128,1024]{1,0:T(8,128)(2,1)}) custom-call(bf16[4096,256]{1,0:T(8,128)(2,1)} %get-tuple-element.27.dq, bf16[4096,128]{1,0:T(8,128)(2,1)} %get-tuple-element.28.dk, bf16[4096,128]{1,0:T(8,128)(2,1)} %get-tuple-element.29.dv), custom_call_target="tpu_custom_call" | custom-call | tf_op jit(solution)/shard_map/collect/pallas_call | solution.py:635
  174.5 2.2 %hand_over.1 = (bf16[128,2048]{1,0:T(8,128)(2,1)}, bf16[128,1024]{1,0:T(8,128)(2,1)}, bf16[128,1024]{1,0:T(8,128)(2,1)}) custom-call(bf16[128,2048]{1,0:T(8,128)(2,1)} %get-tuple-element.30.a, bf16[128,1024]{1,0:T(8,128)(2,1)} %get-tuple-element.31.b, bf16[128,1024]{1,0:T(8,128)(2,1)} %get-tuple-element.32.c), custom_call_target="tpu_custom_call" | custom-call | tf_op jit(solution)/shard_map/hand_over/pallas_call | solution.py:661

commit v5 on v4

--- a/solution.py
+++ b/solution.py
@@ -395,11 +395,11 @@
     relay(EARLY, 1)
     forward(LATE, 1)
     arrive(EARLY)
-    some_tiles(0, 4)
+    some_tiles(0, 2)
     relay(LATE, 0)
-    some_tiles(4, 10)
+    some_tiles(2, 7)
     relay(LATE, 1)
-    some_tiles(10, 16)
+    some_tiles(7, 16)
     arrive(LATE)
 
     for g in range(2):

time: 177 us -> 177 us (level)
  no operation moved by 1% of the time
where the time goes in v5:
time: 177 us
  Pallas kernels  176 us (99%)
    pallas_call x1, Pallas kernels, grads(): pl.pallas_call(functools.partial(grads_kernel, nr, nk), out_shape=(jax.Sh...  60.9 us
    pallas_call x1, Pallas kernels, spread(): pl.pallas_call(spread_kernel, out_shape=(jax.ShapeDtypeStruct((rows, 256)...  53.8 us
    pallas_call x1, Pallas kernels, collect(): pl.pallas_call(collect_kernel, out_shape=(jax.ShapeDtypeStruct((BLK, 2048...  36.7 us
    pallas_call x1, Pallas kernels, totals(): pl.pallas_call(functools.partial(totals_kernel, nr, nk), out_shape=(jax.S...  16.7 us
    pallas_call x1, Pallas kernels, pool(): pl.pallas_call(pool_kernel, out_shape=jax.ShapeDtypeStruct(small, f32), i...  5.85 us

profile of v5, /device:TPU:64, one launch (start us, length us, event | category | flops | bytes accessed | tf_op | source)
XLA Modules:
  0.0 176.8 jit_solution(1172530828113367222)
XLA Ops:
  0.6 53.8 %spread.1 = (bf16[4096,256]{1,0:T(8,128)(2,1)}, bf16[4096,256]{1,0:T(8,128)(2,1)}, bf16[4096,128]{1,0:T(8,128)(2,1)}, bf16[4096,128]{1,0:T(8,128)(2,1)}, f32[4,8...) custom-call(bf16[128,2048]{1,0:T(8,128)(2,1)} %q.1, bf16[128,2048]{1,0:T(8,128)(2,1)} %do.1, ...), custom_call_target="tpu_custom_call" | custom-call | tf_op jit(solution)/shard_map/spread/pallas_call | solution.py:429
  54.4 16.7 %totals.1 = (f32[8,2,8,512]{3,2,1,0:T(8,128)}, s32[72]{0:T(128)}) custom-call(bf16[4096,256]{1,0:T(8,128)(2,1)} %get-tuple-element.18.q_ref, bf16[4096,128]{1,0:T(8,128)(2,1)} %get-tuple-element.19.k_ref, f32[4,8,8,128]{3,2,1,0:T(8,128)} %get-tuple-element.20.aux_r, f32[4,8,8,128]{3,2,1,0:T(8,128)} %get-tuple-element.21.aux_k, ...), custom_call_target="tpu_custom_call" | custom-call | flops 20000000000 | bytes 4194304 | tf_op jit(solution)/shard_map/totals/pallas_call | solution.py:104
  71.2 5.8 %pool.1.z_ref = f32[8,2,512]{2,1,0:T(2,128)} custom-call(f32[8,2,8,512]{3,2,1,0:T(8,128)} %get-tuple-element.26.z), custom_call_target="tpu_custom_call" | custom-call | tf_op jit(solution)/shard_map/pool/pallas_call | solution.py:470
  77.1 60.9 %grads.1 = (bf16[4096,256]{1,0:T(8,128)(2,1)}, bf16[4096,128]{1,0:T(8,128)(2,1)}, bf16[4096,128]{1,0:T(8,128)(2,1)}) custom-call(s32[72]{0:T(128)} %get-tuple-element.23.tiles, bf16[4096,256]{1,0:T(8,128)(2,1)} %get-tuple-element.18.q_ref, bf16[4096,256]{1,0:T(8,128)(2,1)} %get-tuple-element.24.do_ref, bf16[4096,128]{1,0:T(8,128)(2,1)} %get-tuple-element.19.k_ref, ...), custom_call_target="tpu_custom_call" | custom-call | flops 49999998976 | bytes 16777216 | tf_op jit(solution)/shard_map/grads/pallas_call | solution.py:195
  138.0 36.7 %collect.1 = (bf16[128,2048]{1,0:T(8,128)(2,1)}, bf16[128,1024]{1,0:T(8,128)(2,1)}, bf16[128,1024]{1,0:T(8,128)(2,1)}) custom-call(bf16[4096,256]{1,0:T(8,128)(2,1)} %get-tuple-element.27.dq, bf16[4096,128]{1,0:T(8,128)(2,1)} %get-tuple-element.28.dk, bf16[4096,128]{1,0:T(8,128)(2,1)} %get-tuple-element.29.dv), custom_call_target="tpu_custom_call" | custom-call | tf_op jit(solution)/shard_map/collect/pallas_call | solution.py:635
  174.7 2.2 %hand_over.1 = (bf16[128,2048]{1,0:T(8,128)(2,1)}, bf16[128,1024]{1,0:T(8,128)(2,1)}, bf16[128,1024]{1,0:T(8,128)(2,1)}) custom-call(bf16[128,2048]{1,0:T(8,128)(2,1)} %get-tuple-element.30.a, bf16[128,1024]{1,0:T(8,128)(2,1)} %get-tuple-element.31.b, bf16[128,1024]{1,0:T(8,128)(2,1)} %get-tuple-element.32.c), custom_call_target="tpu_custom_call" | custom-call | tf_op jit(solution)/shard_map/hand_over/pallas_call | solution.py:661
